TPU v7x, 32 devices: a whole 2x2x4 slice. The times are simulated.
32 devices in a mesh: blk: 32 (over z, y, x, core).
Axes of the slice: x: 2, y: 2, z: 4, core: 2. Of those that a mesh axis runs over, the one named last changes fastest.
Arguments:
- embeddings: bfloat16 [65536, 1024], P('blk'), may hold values from -400 to 400
- centroid_codes: bfloat16 [16384, 1024], P('blk'), may hold values from -0.1875 to 0.1875
- centroid_scales: bfloat16 [16384], P('blk'), may hold values from 0.5 to 2
- log_normalizers: bfloat16 [65536], P('blk'), may hold values from 1 to 4
Outputs:
- new_centroids: float32 [16384, 1024], P('blk')
- mass_log: float32 [16384], P('blk')
- point_mass: float32 [65536], P('blk')
All inputs are finite; a program needn't handle non-finite values.
Results may differ from a plain program's by a relative error of at most 0.004.
Values may be sent and summed in bfloat16 or wider, within the bound.
No kernel may reach another device: no remote copies, remote signals or barrier semaphores. Data moves between devices by JAX's collectives and lax.ppermute only.
A program may use at most 64 MiB of HBM per device.

v0:
```python
import jax
import jax.numpy as jnp
from jax import lax
from jax.sharding import PartitionSpec as P

STEPS = 2


def from_behind(value, axis, steps):
    count = lax.axis_size(axis)
    pairs = [(source, (source + steps) % count) for source in range(count)]
    return lax.ppermute(value, axis, pairs)


def weigh(unit_rows, log_values, codes, scales):
    similarity = jnp.dot(unit_rows, codes.T, preferred_element_type=jnp.float32)
    weights = jnp.exp(
        similarity * scales.astype(jnp.float32)[None, :] - log_values.astype(jnp.float32)[:, None]
    )
    weights_low = weights.astype(jnp.bfloat16)
    numerator = lax.dot_general(
        weights_low, unit_rows, (((0,), (0,)), ((), ())), preferred_element_type=jnp.float32
    )
    return (numerator, jnp.sum(weights, axis=0), jnp.sum(weights, axis=1))


def on_device(embeddings, centroid_codes, centroid_scales, log_normalizers):
    wide_points = embeddings.astype(jnp.float32)
    unit_rows = (
        wide_points * lax.rsqrt(jnp.mean(wide_points * wide_points, axis=1, keepdims=True) + 1e-06)
    ).astype(jnp.bfloat16)
    numerator, weight_sum, point_total = weigh(
        unit_rows, log_normalizers, centroid_codes, centroid_scales
    )
    moved_codes, moved_scales = (centroid_codes, centroid_scales)
    for offset in range(1, STEPS + 1):
        moved_codes, moved_scales = from_behind((moved_codes, moved_scales), "blk", 1)
        part_numer, part_sum, part_total = weigh(
            unit_rows, log_normalizers, moved_codes, moved_scales
        )
        point_total = point_total + part_total
        numerator, weight_sum = from_behind((numerator, weight_sum), "blk", 1)
        numerator = numerator + part_numer
        weight_sum = weight_sum + part_sum
    numerator, weight_sum = from_behind((numerator, weight_sum), "blk", -STEPS)
    new_centroids = numerator * lax.rsqrt(
        jnp.mean(numerator * numerator, axis=1, keepdims=True) + 1e-06
    )
    return (new_centroids, jnp.log(weight_sum), jnp.log(point_total))


def solution(mesh):
    return jax.shard_map(
        on_device,
        mesh=mesh,
        in_specs=(P("blk", None), P("blk", None), P("blk"), P("blk")),
        out_specs=(P("blk", None), P("blk"), P("blk")),
        check_vma=False,
    )
```

profile of v0, /device:TPU:0, one launch (start us, length us, event | category | flops | bytes accessed | tf_op | source)
XLA Modules:
  0.0 150.4 jit_solution(11137941612577354875)
XLA Ops:
  0.7 3.2 %fusion = f32[2048]{0:T(1024)S(1)} fusion(bf16[2048,1024]{1,0:T(8,128)(2,1)} %param.4), kind=kLoop, calls=%fused_computation.2 | loop fusion | flops 6289408 | bytes 4202496 | tf_op jit(solution)/shard_map/reduce_sum | solution.py:30
  3.9 0.2 copy-done
  4.1 4.4 %fusion.18 = (f32[2048]{0:T(1024)S(1)}, f32[512]{0:T(512)S(1)}, bf16[2048,512]{1,0:T(8,128)(2,1)S(1)}) fusion(f32[2048]{0:T(1024)S(1)} %convert_element_type.32, f32[512]{0:T(512)S(1)} %convert_element_type.31, bf16[512,1024]{1,0:T(8,128)(2,1)} %param.5, bf16[2048,1024]{1,0:T(8,128)(2,1)S(1)} %copy-done, f32[2048]{0:T(1024)S(1)} %add_rsqrt_fusion), kind=kOutput, calls=%fused_computation.20 | convolution fusion | flops 2159015424 | bytes 7368704 | tf_op jit(solution)/shard_map/dot_general | solution.py:16
  8.5 0.0 copy-start.3
  8.5 2.5 %fusion.6 = f32[512,1024]{1,0:T(8,128)S(1)} fusion(bf16[2048,512]{1,0:T(8,128)(2,1)S(1)} %get-tuple-element.9, bf16[2048,1024]{1,0:T(8,128)(2,1)S(1)} %copy-done, f32[2048]{0:T(1024)S(1)} %add_rsqrt_fusion), kind=kOutput, calls=%fused_computation.12 | convolution fusion | flops 2153775104 | bytes 8396800 | tf_op jit(solution)/shard_map/dot_general | solution.py:21
  11.0 0.5 collective-permute-start
  11.5 2.6 %collective-permute-start.1 = (bf16[512,1024]{1,0:T(8,128)(2,1)S(1)}, bf16[512,1024]{1,0:T(8,128)(2,1)S(1)}, u32[]{:S(2)}, u32[]{:S(2)}) collective-permute-start(bf16[512,1024]{1,0:T(8,128)(2,1)S(1)} %copy-done.3), channel_id=1, source_target_pairs={{0,1},{1,2},{2,3},{3,4},{4,5},{5,6},{6,7},{7,8},{8,9},{9,10},{10,1... | collective-permute-start | bytes 3145736 | tf_op jit(solution)/shard_map/ppermute | solution.py:12
  14.1 0.1 collective-permute-start.2
  14.2 38.2 %collective-permute-done.2 = bf16[512]{0:T(512)(128)(2,1)S(1)} collective-permute-done((bf16[512]{0:T(512)(128)(2,1)S(1)}, bf16[512]{0:T(512)(128)(2,1)S(1)}, u32[]{:S(2)}, u32[]{:S(2)}) %collective-permute-start.2) | collective-permute-done | bytes 1056 | tf_op jit(solution)/shard_map/ppermute | solution.py:12
  52.4 0.0 collective-permute-done.1
  52.4 3.2 %fusion.17 = (f32[2048]{0:T(1024)S(1)}, f32[512]{0:T(512)S(1)}, bf16[2048,512]{1,0:T(8,128)(2,1)S(1)}) fusion(f32[2048]{0:T(1024)S(1)} %convert_element_type.32, f32[512]{0:T(512)S(1)} %convert_element_type.34, bf16[512,1024]{1,0:T(8,128)(2,1)S(1)} %collective-permute-done.1, bf16[2048,1024]{1,0:T(8,128)(2,1)S(1)} %copy-done, f32[2048]{0:T(1024)S(1)} %add_rsqrt_fusion), kind=kOutput, calls=%fused_computation.19 | convolution fusion | flops 2159015424 | bytes 7368704 | tf_op jit(solution)/shard_map/dot_general | solution.py:16
  55.6 0.0 collective-permute-done
  55.6 2.5 %fusion.8 = f32[512,1024]{1,0:T(8,128)S(1)} fusion(f32[512,1024]{1,0:T(8,128)S(1)} %collective-permute-done, bf16[2048,512]{1,0:T(8,128)(2,1)S(1)} %get-tuple-element.10, bf16[2048,1024]{1,0:T(8,128)(2,1)S(1)} %copy-done, f32[2048]{0:T(1024)S(1)} %add_rsqrt_fusion), kind=kOutput, calls=%fused_computation.14 | convolution fusion | flops 2154299392 | bytes 10493952 | tf_op jit(solution)/shard_map/dot_general | solution.py:21
  58.1 0.1 collective-permute-start.3
  58.2 0.1 collective-permute-start.5
  58.2 34.5 %collective-permute-done.5 = bf16[512]{0:T(512)(128)(2,1)S(1)} collective-permute-done((bf16[512]{0:T(512)(128)(2,1)S(1)}, bf16[512]{0:T(512)(128)(2,1)S(1)}, u32[]{:S(2)}, u32[]{:S(2)}) %collective-permute-start.5) | collective-permute-done | bytes 1056 | tf_op jit(solution)/shard_map/ppermute | solution.py:12
  92.7 3.1 %fusion.19 = (f32[2048]{0:T(1024)S(1)}, f32[512]{0:T(512)S(1)}, bf16[2048,512]{1,0:T(8,128)(2,1)S(1)}) fusion(f32[2048]{0:T(1024)S(1)} %convert_element_type.32, f32[512]{0:T(512)S(1)} %convert_element_type.36, bf16[512,1024]{1,0:T(8,128)(2,1)S(1)} %collective-permute-done.4, bf16[2048,1024]{1,0:T(8,128)(2,1)S(1)} %copy-done, f32[2048]{0:T(1024)S(1)} %add_rsqrt_fusion), kind=kOutput, calls=%fused_computation.21 | convolution fusion | flops 2159015424 | bytes 7368704 | tf_op jit(solution)/shard_map/dot_general | solution.py:16
  95.9 2.5 %fusion.2 = f32[512,1024]{1,0:T(8,128)S(1)} fusion(bf16[2048,512]{1,0:T(8,128)(2,1)S(1)} %get-tuple-element.11, bf16[2048,1024]{1,0:T(8,128)(2,1)S(1)} %copy-done, f32[2048]{0:T(1024)S(1)} %add_rsqrt_fusion), kind=kOutput, calls=%fused_computation.8 | convolution fusion | flops 2153775104 | bytes 8396800 | tf_op jit(solution)/shard_map/dot_general | solution.py:21
  98.4 0.0 collective-permute-done.3
  98.4 0.4 add.43
  98.8 0.1 collective-permute-start.6
  98.9 0.1 collective-permute-start.7
  98.9 6.7 %collective-permute-done.7 = f32[512]{0:T(512)S(1)} collective-permute-done((f32[512]{0:T(512)S(1)}, f32[512]{0:T(512)S(1)}, u32[]{:S(2)}, u32[]{:S(2)}) %collective-permute-start.7) | collective-permute-done | bytes 2080 | tf_op jit(solution)/shard_map/ppermute | solution.py:12
  105.6 0.0 collective-permute-start.8
  105.6 6.7 %collective-permute-done.8 = f32[512]{0:T(512)S(1)} collective-permute-done((f32[512]{0:T(512)S(1)}, f32[512]{0:T(512)S(1)}, u32[]{:S(2)}, u32[]{:S(2)}) %collective-permute-start.8) | collective-permute-done | bytes 2080 | tf_op jit(solution)/shard_map/ppermute | solution.py:12
  112.3 34.4 %collective-permute-start.9 = (f32[512]{0:T(512)S(1)}, f32[512]{0:T(512)S(1)}, u32[]{:S(2)}, u32[]{:S(2)}) collective-permute-start(f32[512]{0:T(512)S(1)} %add.47), channel_id=1, source_target_pairs={{0,30},{1,31},{2,0},{3,1},{4,2},{5,3},{6,4},{7,5},{8,6},{9,7},{10,... | collective-permute-start | bytes 6152 | tf_op jit(solution)/shard_map/ppermute | solution.py:12
  146.7 0.6 add_log_fusion
  147.3 0.7 collective-permute-done.9
  148.0 0.6 log.6
  148.6 0.0 collective-permute-done.6
  148.6 0.2 multiply_reduce_fusion
  148.8 1.5 %broadcast_multiply_fusion = f32[512,1024]{1,0:T(8,128)} fusion(f32[512,1024]{1,0:T(8,128)S(1)} %collective-permute-done.6, f32[512]{0:T(512)S(1)} %add_rsqrt_fusion.1), kind=kLoop, calls=%fused_computation.15 | loop fusion | flops 524288 | bytes 4196352 | tf_op jit(solution)/shard_map/mul | solution.py:46
  (16 shorter events, 0.1 us)
Async XLA Ops:
  0.6 3.5 %copy-start = (bf16[2048,1024]{1,0:T(8,128)(2,1)S(1)}, bf16[2048,1024]{1,0:T(8,128)(2,1)}, u32[]{:S(2)}) copy-start(bf16[2048,1024]{1,0:T(8,128)(2,1)} %param.4) | copy-start | bytes 12582916
  0.6 3.3 %copy-start.1 = (bf16[2048]{0:T(1024)(128)(2,1)S(1)}, bf16[2048]{0:T(1024)(128)(2,1)}, u32[]{:S(2)}) copy-start(bf16[2048]{0:T(1024)(128)(2,1)} %param.7) | copy-start | bytes 12292
  0.7 3.3 %copy-start.2 = (bf16[512]{0:T(512)(128)(2,1)S(1)}, bf16[512]{0:T(512)(128)(2,1)}, u32[]{:S(2)}) copy-start(bf16[512]{0:T(512)(128)(2,1)} %param.6) | copy-start | bytes 3076
  8.5 3.0 %copy-start.3 = (bf16[512,1024]{1,0:T(8,128)(2,1)S(1)}, bf16[512,1024]{1,0:T(8,128)(2,1)}, u32[]{:S(2)}) copy-start(bf16[512,1024]{1,0:T(8,128)(2,1)} %param.5) | copy-start | bytes 3145732
  11.0 44.6 %collective-permute-start = (f32[512,1024]{1,0:T(8,128)S(1)}, f32[512,1024]{1,0:T(8,128)S(1)}, u32[]{:S(2)}, u32[]{:S(2)}) collective-permute-start(f32[512,1024]{1,0:T(8,128)S(1)} %fusion.6), channel_id=1, source_target_pairs={{0,1},{1,2},{2,3},{3,4},{4,5},{5,6},{6,7},{7,8},{8,9},{9,10},{10,1... | collective-permute-start | bytes 6291464 | tf_op jit(solution)/shard_map/ppermute | solution.py:12
  11.5 40.9 %collective-permute-start.1 = (bf16[512,1024]{1,0:T(8,128)(2,1)S(1)}, bf16[512,1024]{1,0:T(8,128)(2,1)S(1)}, u32[]{:S(2)}, u32[]{:S(2)}) collective-permute-start(bf16[512,1024]{1,0:T(8,128)(2,1)S(1)} %copy-done.3), channel_id=1, source_target_pairs={{0,1},{1,2},{2,3},{3,4},{4,5},{5,6},{6,7},{7,8},{8,9},{9,10},{10,1... | collective-permute-start | bytes 3145736 | tf_op jit(solution)/shard_map/ppermute | solution.py:12
  14.1 38.3 %collective-permute-start.2 = (bf16[512]{0:T(512)(128)(2,1)S(1)}, bf16[512]{0:T(512)(128)(2,1)S(1)}, u32[]{:S(2)}, u32[]{:S(2)}) collective-permute-start(bf16[512]{0:T(512)(128)(2,1)S(1)} %copy-done.2), channel_id=1, source_target_pairs={{0,1},{1,2},{2,3},{3,4},{4,5},{5,6},{6,7},{7,8},{8,9},{9,10},{10,1... | collective-permute-start | bytes 3080 | tf_op jit(solution)/shard_map/ppermute | solution.py:12
  52.4 40.3 %collective-permute-start.4 = (bf16[512,1024]{1,0:T(8,128)(2,1)S(1)}, bf16[512,1024]{1,0:T(8,128)(2,1)S(1)}, u32[]{:S(2)}, u32[]{:S(2)}) collective-permute-start(bf16[512,1024]{1,0:T(8,128)(2,1)S(1)} %collective-permute-done.1), channel_id=1, source_target_pairs={{0,1},{1,2},{2,3},{3,4},{4,5},{5,6},{6,7},{7,8},{8,9},{9,10},{10,1... | collective-permute-start | bytes 3145736 | tf_op jit(solution)/shard_map/ppermute | solution.py:12
  58.1 40.3 %collective-permute-start.3 = (f32[512,1024]{1,0:T(8,128)S(1)}, f32[512,1024]{1,0:T(8,128)S(1)}, u32[]{:S(2)}, u32[]{:S(2)}) collective-permute-start(f32[512,1024]{1,0:T(8,128)S(1)} %fusion.8), channel_id=1, source_target_pairs={{0,1},{1,2},{2,3},{3,4},{4,5},{5,6},{6,7},{7,8},{8,9},{9,10},{10,1... | collective-permute-start | bytes 6291464 | tf_op jit(solution)/shard_map/ppermute | solution.py:12
  58.2 34.6 %collective-permute-start.5 = (bf16[512]{0:T(512)(128)(2,1)S(1)}, bf16[512]{0:T(512)(128)(2,1)S(1)}, u32[]{:S(2)}, u32[]{:S(2)}) collective-permute-start(bf16[512]{0:T(512)(128)(2,1)S(1)} %collective-permute-done.2), channel_id=1, source_target_pairs={{0,1},{1,2},{2,3},{3,4},{4,5},{5,6},{6,7},{7,8},{8,9},{9,10},{10,1... | collective-permute-start | bytes 3080 | tf_op jit(solution)/shard_map/ppermute | solution.py:12
  98.8 49.8 %collective-permute-start.6 = (f32[512,1024]{1,0:T(8,128)S(1)}, f32[512,1024]{1,0:T(8,128)S(1)}, u32[]{:S(2)}, u32[]{:S(2)}) collective-permute-start(f32[512,1024]{1,0:T(8,128)S(1)} %add.43), channel_id=1, source_target_pairs={{0,30},{1,31},{2,0},{3,1},{4,2},{5,3},{6,4},{7,5},{8,6},{9,7},{10,... | collective-permute-start | bytes 6291464 | tf_op jit(solution)/shard_map/ppermute | solution.py:12
  98.9 6.8 %collective-permute-start.7 = (f32[512]{0:T(512)S(1)}, f32[512]{0:T(512)S(1)}, u32[]{:S(2)}, u32[]{:S(2)}) collective-permute-start(f32[512]{0:T(512)S(1)} %get-tuple-element.6), channel_id=1, source_target_pairs={{0,1},{1,2},{2,3},{3,4},{4,5},{5,6},{6,7},{7,8},{8,9},{9,10},{10,1... | collective-permute-start | bytes 6152 | tf_op jit(solution)/shard_map/ppermute | solution.py:12
  105.6 6.7 %collective-permute-start.8 = (f32[512]{0:T(512)S(1)}, f32[512]{0:T(512)S(1)}, u32[]{:S(2)}, u32[]{:S(2)}) collective-permute-start(f32[512]{0:T(512)S(1)} %add.46), channel_id=1, source_target_pairs={{0,1},{1,2},{2,3},{3,4},{4,5},{5,6},{6,7},{7,8},{8,9},{9,10},{10,1... | collective-permute-start | bytes 6152 | tf_op jit(solution)/shard_map/ppermute | solution.py:12
  112.3 35.7 %collective-permute-start.9 = (f32[512]{0:T(512)S(1)}, f32[512]{0:T(512)S(1)}, u32[]{:S(2)}, u32[]{:S(2)}) collective-permute-start(f32[512]{0:T(512)S(1)} %add.47), channel_id=1, source_target_pairs={{0,30},{1,31},{2,0},{3,1},{4,2},{5,3},{6,4},{7,5},{8,6},{9,7},{10,... | collective-permute-start | bytes 6152 | tf_op jit(solution)/shard_map/ppermute | solution.py:12
where the time goes:
time: 151 us; the launch traced here: 150 us
  waiting for transfers between devices  86.9 us (58%)
  starting transfers between devices  37.8 us (25%)
  matrix products  18.1 us (12%)
  other arithmetic  6.01 us (4%)
    ppermute x10, waiting for transfers between devices, from_behind(): return lax.ppermute(value, axis, pairs)  86.9 us
    ppermute x10, starting transfers between devices, from_behind(): return lax.ppermute(value, axis, pairs)  37.8 us
    dot_general x3, matrix products, weigh(): similarity = jnp.dot(unit_rows, codes.T, preferred_element_type=jnp.float32)  10.7 us
    dot_general x3, matrix products, weigh(): lax.dot_general(weights_low, unit_rows, (((0,), (0,)), ((), ())), preferr...  7.46 us
    reduce_sum x1, other arithmetic, on_device(): jnp.mean(wide_points * wide_points, axis=1, keepdims=True) + 1e-06  3.22 us
  transfers between devices with their start and end apart: 10, of which 5 were waited for; matrix products, arithmetic and copies ran while one was open for 8% of the time, Pallas kernels for 0%

commit v1 on v0

v1 whole, which is shorter than its diff:
```python
import jax
import jax.numpy as jnp
from jax import lax
from jax.sharding import PartitionSpec as P

PARTS = 2
EXTRA = 16


def shift(value, steps):
    count = lax.axis_size("blk")
    return lax.ppermute(value, "blk", [(i, (i + steps) % count) for i in range(count)])


def partner(value):
    count = lax.axis_size("blk")
    return lax.ppermute(value, "blk", [(i, i ^ 1) for i in range(count)])


def weigh(unit_rows, log_values, codes, scales):
    similarity = jnp.dot(unit_rows, codes.T, preferred_element_type=jnp.float32)
    weights = jnp.exp(similarity * scales[None, :] - log_values[:, None])
    numerator = lax.dot_general(
        weights.astype(jnp.bfloat16),
        unit_rows,
        (((0,), (0,)), ((), ())),
        preferred_element_type=jnp.float32,
    )
    return numerator, jnp.sum(weights, axis=0), jnp.sum(weights, axis=1)


def on_device(embeddings, centroid_codes, centroid_scales, log_normalizers):
    odd = lax.axis_index("blk") % 2 == 1
    rows, width = centroid_codes.shape
    part = rows // PARTS
    scale_rows = jnp.pad(centroid_scales[None, :], ((0, EXTRA - 1), (0, width - rows)))
    received = []
    for k in range(PARTS):
        block = centroid_codes[k * part : (k + 1) * part]
        if k == 0:
            block = jnp.concatenate([block, scale_rows], axis=0)
        received.append(shift(block, 2))
    wide = embeddings.astype(jnp.float32)
    unit_rows = (
        wide * lax.rsqrt(jnp.mean(wide * wide, axis=1, keepdims=True) + 1e-06)
    ).astype(jnp.bfloat16)
    logs = log_normalizers.astype(jnp.float32)
    other_rows = partner(unit_rows)
    other_logs = partner(log_normalizers).astype(jnp.float32)
    scales = centroid_scales.astype(jnp.float32)
    own_numer, own_sum, point_total = weigh(unit_rows, logs, centroid_codes, scales)
    moved_scales = received[0][part, :rows].astype(jnp.float32)
    other_total = 0.0
    own_numers, own_sums, sent = [], [], []
    for k in range(PARTS):
        cut = slice(k * part, (k + 1) * part)
        codes = received[k][:part]
        numer, total, points = weigh(unit_rows, logs, codes, moved_scales[cut])
        numer2, total2, points2 = weigh(
            other_rows,
            other_logs,
            jnp.where(odd, codes, centroid_codes[cut]),
            jnp.where(odd, moved_scales[cut], scales[cut]),
        )
        point_total = point_total + points
        other_total = other_total + points2
        numer = numer + jnp.where(odd, numer2, 0.0)
        total = total + jnp.where(odd, total2, 0.0)
        own_numers.append(own_numer[cut] + jnp.where(odd, 0.0, numer2))
        own_sums.append(own_sum[cut] + jnp.where(odd, 0.0, total2))
        high = total.astype(jnp.bfloat16)
        low = (total - high.astype(jnp.float32)).astype(jnp.bfloat16)
        ends = jnp.pad(jnp.stack([high, low]), ((0, EXTRA - 2), (0, width - part)))
        sent.append(shift(jnp.concatenate([numer.astype(jnp.bfloat16), ends], axis=0), -2))
    point_total = point_total + partner(other_total)
    outs, sums = [], []
    for k in range(PARTS):
        back = sent[k].astype(jnp.float32)
        numer = own_numers[k] + back[:part]
        outs.append(numer * lax.rsqrt(jnp.mean(numer * numer, axis=1, keepdims=True) + 1e-06))
        sums.append(own_sums[k] + (back[part, :part] + back[part + 1, :part]))
    return (
        jnp.concatenate(outs, axis=0),
        jnp.log(jnp.concatenate(sums)),
        jnp.log(point_total),
    )


def solution(mesh):
    return jax.shard_map(
        on_device,
        mesh=mesh,
        in_specs=(P("blk", None), P("blk", None), P("blk"), P("blk")),
        out_specs=(P("blk", None), P("blk"), P("blk")),
        check_vma=False,
    )
```

time: 151 us -> 90.9 us (0.60)
  waiting for transfers between devices: 86.9 us -> 31.3 us
  starting transfers between devices: 37.8 us -> 8.57 us
  matrix products: 18.1 us -> 39.8 us
  other arithmetic: 6.01 us -> 9.63 us
    ppermute x10 -> x7, waiting for transfers between devices: 86.9 us -> 31.3 us  [the longest x4 31.3 us: shift(): lax.ppermute(value, 'blk', [(i, (i + steps) % count) for i in range(count)])]
    ppermute x10 -> x7, starting transfers between devices: 37.8 us -> 8.57 us  [the longest x4 7.99 us: shift(): lax.ppermute(value, 'blk', [(i, (i + steps) % count) for i in range(count)])]
    dot_general x3 -> x5, matrix products: 7.46 us -> 18.5 us  [weigh(): lax.dot_general(weights.astype(jnp.bfloat16), unit_rows, (((0,), (0,)), (...]
    dot_general x3 -> x5, matrix products: 10.7 us -> 21.3 us  [weigh(): similarity = jnp.dot(unit_rows, codes.T, preferred_element_type=jnp.float32)]
    convert_element_type x4 -> x11, other arithmetic: 0.01 us -> 2.92 us  [the longest x1 2.67 us: on_device(): unit_rows = (wide * lax.rsqrt(jnp.mean(wide * wide, axis=1, keepdims=True...]
    concatenate x0 -> x4, other arithmetic: none -> 1.57 us  [the longest x1 1.46 us: on_device(): jnp.concatenate(outs, axis=0)]
  transfers between devices with their start and end apart: 10 -> 7, of which waited for: 5 -> 2; matrix products, arithmetic and copies ran while one was open for 8% -> 37% of each run, Pallas kernels for 0% -> 0%
where the time goes in v1:
time: 90.9 us; the launch traced here: 90.5 us
  matrix products  39.8 us (44%)
  waiting for transfers between devices  31.3 us (34%)
  other arithmetic  9.63 us (11%)
  starting transfers between devices  8.57 us (9%)
    ppermute x4, waiting for transfers between devices, shift(): lax.ppermute(value, 'blk', [(i, (i + steps) % count) for i in range(count)])  31.3 us
    dot_general x5, matrix products, weigh(): similarity = jnp.dot(unit_rows, codes.T, preferred_element_type=jnp.float32)  21.3 us
    dot_general x5, matrix products, weigh(): lax.dot_general(weights.astype(jnp.bfloat16), unit_rows, (((0,), (0,)), (...  18.5 us
    ppermute x4, starting transfers between devices, shift(): lax.ppermute(value, 'blk', [(i, (i + steps) % count) for i in range(count)])  7.99 us
    reduce_sum x1, other arithmetic, on_device(): jnp.mean(wide * wide, axis=1, keepdims=True) + 1e-06  3.22 us
    convert_element_type x1, other arithmetic, on_device(): unit_rows = (wide * lax.rsqrt(jnp.mean(wide * wide, axis=1, keepdims=True...  2.67 us
  transfers between devices with their start and end apart: 7, of which 2 were waited for; matrix products, arithmetic and copies ran while one was open for 37% of the time, Pallas kernels for 0%

profile of v1, /device:TPU:0, one launch (start us, length us, event | category | flops | bytes accessed | tf_op | source)
XLA Modules:
  0.0 90.5 jit_solution(14424026956173497550)
XLA Ops:
  0.6 3.2 %fusion = f32[2048]{0:T(1024)S(1)} fusion(bf16[2048,1024]{1,0:T(8,128)(2,1)} %param.4), kind=kLoop, calls=%fused_computation.2 | loop fusion | flops 6289408 | bytes 4202496 | tf_op jit(solution)/shard_map/reduce_sum | solution.py:45
  3.9 0.2 copy-done
  4.1 2.7 %fusion.1 = bf16[2048,1024]{1,0:T(8,128)(2,1)} fusion(bf16[2048,1024]{1,0:T(8,128)(2,1)S(1)} %copy-done, f32[2048]{0:T(1024)S(1)} %add_rsqrt_fusion), kind=kLoop, calls=%fused_computation.3 | loop fusion | flops 6291456 | bytes 8396800 | tf_op jit(solution)/shard_map/convert_element_type | solution.py:46
  6.8 0.5 collective-permute-start
  7.2 0.1 collective-permute-start.2
  7.3 0.1 fusion.50
  7.3 3.0 %collective-permute-start.4 = (bf16[256,1024]{1,0:T(8,128)(2,1)S(1)}, bf16[256,1024]{1,0:T(8,128)(2,1)S(1)}, u32[]{:S(2)}, u32[]{:S(2)}) collective-permute-start(bf16[256,1024]{1,0:T(8,128)(2,1)S(1)} %get-tuple-element.20), channel_id=1, source_target_pairs={{0,2},{1,3},{2,4},{3,5},{4,6},{5,7},{6,8},{7,9},{8,10},{9,11},{10,... | collective-permute-start | bytes 1572872 | tf_op jit(solution)/shard_map/ppermute | solution.py:12
  10.4 1.5 %collective-permute-start.1 = (bf16[272,1024]{1,0:T(8,128)(2,1)S(1)}, bf16[272,1024]{1,0:T(8,128)(2,1)S(1)}, u32[]{:S(2)}, u32[]{:S(2)}) collective-permute-start(bf16[272,1024]{1,0:T(8,128)(2,1)S(1)} %fusion.25), channel_id=1, source_target_pairs={{0,2},{1,3},{2,4},{3,5},{4,6},{5,7},{6,8},{7,9},{8,10},{9,11},{10,... | collective-permute-start | bytes 1671176 | tf_op jit(solution)/shard_map/ppermute | solution.py:12
  11.9 6.5 %fusion.45 = (f32[2048]{0:T(1024)S(1)}, f32[512]{0:T(512)S(1)}, bf16[2048,512]{1,0:T(8,128)(2,1)}) fusion(f32[2048]{0:T(1024)S(1)} %convert_element_type.122, f32[512]{0:T(512)S(1)} %convert_element_type.121, bf16[2048,1024]{1,0:T(8,128)(2,1)} %fusion.1, bf16[512,1024]{1,0:T(8,128)(2,1)S(1)} %copy-done.1), kind=kOutput, calls=%fused_computation.80 | convolution fusion | flops 2152723968 | bytes 7360512 | tf_op jit(solution)/shard_map/dot_general | solution.py:21
  18.4 20.0 %collective-permute-done.1 = bf16[272,1024]{1,0:T(8,128)(2,1)S(1)} collective-permute-done((bf16[272,1024]{1,0:T(8,128)(2,1)S(1)}, bf16[272,1024]{1,0:T(8,128)(2,1)S(1)}, u32[]{:S(2)}, u32[]{:S(2)}) %collective-permute-start.1) | collective-permute-done | bytes 557088 | tf_op jit(solution)/shard_map/ppermute | solution.py:12
  38.4 0.0 collective-permute-done.4
  38.4 3.7 %fusion.47 = (f32[2048]{0:T(1024)S(1)}, f32[256]{0:T(256)S(1)}, bf16[2048,256]{1,0:T(8,128)(2,1)S(1)}) fusion(f32[2048]{0:T(1024)S(1)} %convert_element_type.122, f32[256]{0:T(256)S(1)} %bitcast.32, bf16[2048,1024]{1,0:T(8,128)(2,1)} %fusion.1, bf16[256,1024]{1,0:T(8,128)(2,1)S(1)} %collective-permute-done.4), kind=kOutput, calls=%fused_computation.82 | convolution fusion | flops 1076360960 | bytes 5785600 | tf_op jit(solution)/shard_map/dot_general | solution.py:21
  42.1 3.7 %fusion.46 = (f32[2048]{0:T(1024)S(1)}, f32[256]{0:T(256)S(1)}, bf16[2048,256]{1,0:T(8,128)(2,1)S(1)}) fusion(f32[2048]{0:T(1024)S(1)} %convert_element_type.122, f32[256]{0:T(256)S(1)} %bitcast.30, bf16[2048,1024]{1,0:T(8,128)(2,1)} %fusion.1, bf16[272,1024]{1,0:T(8,128)(2,1)S(1)} %collective-permute-done.1), kind=kOutput, calls=%fused_computation.81 | convolution fusion | flops 1076360960 | bytes 5785600 | tf_op jit(solution)/shard_map/dot_general | solution.py:21
  45.8 3.7 %fusion.49 = (f32[2048]{0:T(1024)S(1)}, f32[256]{0:T(256)S(1)}, bf16[2048,256]{1,0:T(8,128)(2,1)S(1)}) fusion(f32[2048]{0:T(1024)S(1)} %convert_element_type.125, f32[256]{0:T(256)S(1)} %get-tuple-element.23, bf16[2048,1024]{1,0:T(8,128)(2,1)} %collective-permute-done, pred[]{:T(512)S(6)} %eq.5, bf16[272,1024]{1,0:T(8,128)(2,1)S(1)} %collective-permute-done.1, ...), kind=kOutput, calls=%fused_computation.84 | convolution fusion | flops 1076623104 | bytes 6309889 | tf_op jit(solution)/shard_map/dot_general | solution.py:21
  49.6 3.7 %fusion.48 = (f32[2048]{0:T(1024)S(1)}, f32[256]{0:T(256)S(1)}, bf16[2048,256]{1,0:T(8,128)(2,1)S(1)}) fusion(f32[2048]{0:T(1024)S(1)} %convert_element_type.125, f32[256]{0:T(256)S(1)} %get-tuple-element.24, bf16[2048,1024]{1,0:T(8,128)(2,1)} %collective-permute-done, bf16[256,1024]{1,0:T(8,128)(2,1)S(1)} %collective-permute-done.4, pred[]{:T(512)S(6)} %eq.5, ...), kind=kOutput, calls=%fused_computation.83 | convolution fusion | flops 1076623104 | bytes 6309889 | tf_op jit(solution)/shard_map/dot_general | solution.py:21
  53.3 0.1 collective-permute-start.6
  53.4 3.5 %fusion.23 = f32[256,1024]{1,0:T(8,128)S(1)} fusion(bf16[2048,1024]{1,0:T(8,128)(2,1)} %collective-permute-done, bf16[2048,256]{1,0:T(8,128)(2,1)S(1)} %get-tuple-element.28), kind=kOutput, calls=%fused_computation.36 | convolution fusion | flops 1073741824 | bytes 6291456 | tf_op jit(solution)/shard_map/dot_general | solution.py:23
  56.9 3.5 %add_convert_fusion.1 = bf16[256,1024]{1,0:T(8,128)(2,1)S(1)} fusion(f32[256,1024]{1,0:T(8,128)S(1)} %fusion.23, bf16[2048,1024]{1,0:T(8,128)(2,1)} %fusion.1, bf16[2048,256]{1,0:T(8,128)(2,1)S(1)} %get-tuple-element.27, pred[]{:T(512)S(6)} %eq.5), kind=kOutput, calls=%fused_computation.33 | convolution fusion | flops 1074528256 | bytes 6815745 | tf_op jit(solution)/shard_map/dot_general | solution.py:23
  60.4 2.0 %collective-permute-start.3 = (bf16[272,1024]{1,0:T(8,128)(2,1)S(1)}, bf16[272,1024]{1,0:T(8,128)(2,1)S(1)}, u32[]{:S(2)}, u32[]{:S(2)}) collective-permute-start(bf16[272,1024]{1,0:T(8,128)(2,1)S(1)} %pad_maximum_fusion.1), channel_id=1, source_target_pairs={{0,30},{1,31},{2,0},{3,1},{4,2},{5,3},{6,4},{7,5},{8,6},{9,7},{10,... | collective-permute-start | bytes 1671176 | tf_op jit(solution)/shard_map/ppermute | solution.py:12
  62.4 3.5 %fusion.17 = f32[256,1024]{1,0:T(8,128)S(1)} fusion(bf16[2048,1024]{1,0:T(8,128)(2,1)} %collective-permute-done, bf16[2048,256]{1,0:T(8,128)(2,1)S(1)} %get-tuple-element.30), kind=kOutput, calls=%fused_computation.30 | convolution fusion | flops 1073741824 | bytes 6291456 | tf_op jit(solution)/shard_map/dot_general | solution.py:23
  65.9 0.0 copy-start.4
  65.9 3.6 %add_convert_fusion = bf16[256,1024]{1,0:T(8,128)(2,1)S(1)} fusion(f32[256,1024]{1,0:T(8,128)S(1)} %fusion.17, bf16[2048,1024]{1,0:T(8,128)(2,1)} %fusion.1, bf16[2048,256]{1,0:T(8,128)(2,1)S(1)} %get-tuple-element.29, pred[]{:T(512)S(6)} %eq.5), kind=kOutput, calls=%fused_computation.27 | convolution fusion | flops 1074528256 | bytes 6815745 | tf_op jit(solution)/shard_map/dot_general | solution.py:23
  69.5 1.5 %collective-permute-start.5 = (bf16[272,1024]{1,0:T(8,128)(2,1)S(1)}, bf16[272,1024]{1,0:T(8,128)(2,1)S(1)}, u32[]{:S(2)}, u32[]{:S(2)}) collective-permute-start(bf16[272,1024]{1,0:T(8,128)(2,1)S(1)} %pad_maximum_fusion.2), channel_id=1, source_target_pairs={{0,30},{1,31},{2,0},{3,1},{4,2},{5,3},{6,4},{7,5},{8,6},{9,7},{10,... | collective-permute-start | bytes 1671176 | tf_op jit(solution)/shard_map/ppermute | solution.py:12
  71.0 4.5 %fusion.10 = f32[512,1024]{1,0:T(8,128)S(1)} fusion(bf16[2048,1024]{1,0:T(8,128)(2,1)} %fusion.1, bf16[2048,512]{1,0:T(8,128)(2,1)S(1)} %copy-done.4), kind=kOutput, calls=%fused_computation.18 | convolution fusion | flops 2147483648 | bytes 8388608 | tf_op jit(solution)/shard_map/dot_general | solution.py:23
  75.6 0.6 add_log_fusion
  76.2 0.1 convert_element_type.132
  76.3 11.3 %collective-permute-done.5 = bf16[272,1024]{1,0:T(8,128)(2,1)S(1)} collective-permute-done((bf16[272,1024]{1,0:T(8,128)(2,1)S(1)}, bf16[272,1024]{1,0:T(8,128)(2,1)S(1)}, u32[]{:S(2)}, u32[]{:S(2)}) %collective-permute-start.5) | collective-permute-done | bytes 557088 | tf_op jit(solution)/shard_map/ppermute | solution.py:12
  87.6 0.1 convert_element_type.139
  87.7 0.4 multiply_reduce_fusion.1
  88.2 0.6 maximum_log_fusion
  88.8 0.2 broadcast_multiply_fusion
  89.0 1.5 %pad_maximum_fusion = f32[512,1024]{1,0:T(8,128)} fusion(f32[256,1024]{1,0:T(8,128)S(1)} %get-tuple-element.32, f32[256,1024]{1,0:T(8,128)S(1)} %get-tuple-element.33), kind=kLoop, calls=%fused_computation.17 | loop fusion | flops 524288 | bytes 4194304 | tf_op jit(solution)/shard_map/concatenate | solution.py:83
  (37 shorter events, 0.3 us)
Async XLA Ops:
  0.6 3.5 %copy-start = (bf16[2048,1024]{1,0:T(8,128)(2,1)S(1)}, bf16[2048,1024]{1,0:T(8,128)(2,1)}, u32[]{:S(2)}) copy-start(bf16[2048,1024]{1,0:T(8,128)(2,1)} %param.4) | copy-start | bytes 12582916
  4.1 3.1 %copy-start.2 = (bf16[2048]{0:T(1024)(128)(2,1)S(1)}, bf16[2048]{0:T(1024)(128)(2,1)}, u32[]{:S(2)}) copy-start(bf16[2048]{0:T(1024)(128)(2,1)} %param.7) | copy-start | bytes 12292
  4.1 3.2 %copy-start.1 = (bf16[512,1024]{1,0:T(8,128)(2,1)S(1)}, bf16[512,1024]{1,0:T(8,128)(2,1)}, u32[]{:S(2)}) copy-start(bf16[512,1024]{1,0:T(8,128)(2,1)} %param.5) | copy-start | bytes 3145732
  6.8 3.6 %copy-start.3 = (bf16[512]{0:T(512)(128)(2,1)S(1)}, bf16[512]{0:T(512)(128)(2,1)}, u32[]{:S(2)}) copy-start(bf16[512]{0:T(512)(128)(2,1)} %param.6) | copy-start | bytes 3076
  6.8 39.1 %collective-permute-start = (bf16[2048,1024]{1,0:T(8,128)(2,1)}, bf16[2048,1024]{1,0:T(8,128)(2,1)}, u32[]{:S(2)}, u32[]{:S(2)}) collective-permute-start(bf16[2048,1024]{1,0:T(8,128)(2,1)} %fusion.1), channel_id=1, source_target_pairs={{0,1},{1,0},{2,3},{3,2},{4,5},{5,4},{6,7},{7,6},{8,9},{9,8},{10,11... | collective-permute-start | bytes 12582920 | tf_op jit(solution)/shard_map/ppermute | solution.py:17
  7.2 11.2 %collective-permute-start.2 = (bf16[2048]{0:T(1024)(128)(2,1)S(1)}, bf16[2048]{0:T(1024)(128)(2,1)S(1)}, u32[]{:S(2)}, u32[]{:S(2)}) collective-permute-start(bf16[2048]{0:T(1024)(128)(2,1)S(1)} %copy-done.2), channel_id=1, source_target_pairs={{0,1},{1,0},{2,3},{3,2},{4,5},{5,4},{6,7},{7,6},{8,9},{9,8},{10,11... | collective-permute-start | bytes 12296 | tf_op jit(solution)/shard_map/ppermute | solution.py:17
  7.3 31.1 %collective-permute-start.4 = (bf16[256,1024]{1,0:T(8,128)(2,1)S(1)}, bf16[256,1024]{1,0:T(8,128)(2,1)S(1)}, u32[]{:S(2)}, u32[]{:S(2)}) collective-permute-start(bf16[256,1024]{1,0:T(8,128)(2,1)S(1)} %get-tuple-element.20), channel_id=1, source_target_pairs={{0,2},{1,3},{2,4},{3,5},{4,6},{5,7},{6,8},{7,9},{8,10},{9,11},{10,... | collective-permute-start | bytes 1572872 | tf_op jit(solution)/shard_map/ppermute | solution.py:12
  10.4 28.0 %collective-permute-start.1 = (bf16[272,1024]{1,0:T(8,128)(2,1)S(1)}, bf16[272,1024]{1,0:T(8,128)(2,1)S(1)}, u32[]{:S(2)}, u32[]{:S(2)}) collective-permute-start(bf16[272,1024]{1,0:T(8,128)(2,1)S(1)} %fusion.25), channel_id=1, source_target_pairs={{0,2},{1,3},{2,4},{3,5},{4,6},{5,7},{6,8},{7,9},{8,10},{9,11},{10,... | collective-permute-start | bytes 1671176 | tf_op jit(solution)/shard_map/ppermute | solution.py:12
  53.3 22.2 %collective-permute-start.6 = (f32[2048]{0:T(1024)S(1)}, f32[2048]{0:T(1024)S(1)}, u32[]{:S(2)}, u32[]{:S(2)}) collective-permute-start(f32[2048]{0:T(1024)S(1)} %add.150), channel_id=1, source_target_pairs={{0,1},{1,0},{2,3},{3,2},{4,5},{5,4},{6,7},{7,6},{8,9},{9,8},{10,11... | collective-permute-start | bytes 24584 | tf_op jit(solution)/shard_map/ppermute | solution.py:17
  60.4 15.8 %collective-permute-start.3 = (bf16[272,1024]{1,0:T(8,128)(2,1)S(1)}, bf16[272,1024]{1,0:T(8,128)(2,1)S(1)}, u32[]{:S(2)}, u32[]{:S(2)}) collective-permute-start(bf16[272,1024]{1,0:T(8,128)(2,1)S(1)} %pad_maximum_fusion.1), channel_id=1, source_target_pairs={{0,30},{1,31},{2,0},{3,1},{4,2},{5,3},{6,4},{7,5},{8,6},{9,7},{10,... | collective-permute-start | bytes 1671176 | tf_op jit(solution)/shard_map/ppermute | solution.py:12
  65.9 5.1 %copy-start.4 = (bf16[2048,512]{1,0:T(8,128)(2,1)S(1)}, bf16[2048,512]{1,0:T(8,128)(2,1)}, u32[]{:S(2)}) copy-start(bf16[2048,512]{1,0:T(8,128)(2,1)} %get-tuple-element.31) | copy-start | bytes 6291460
  69.5 18.1 %collective-permute-start.5 = (bf16[272,1024]{1,0:T(8,128)(2,1)S(1)}, bf16[272,1024]{1,0:T(8,128)(2,1)S(1)}, u32[]{:S(2)}, u32[]{:S(2)}) collective-permute-start(bf16[272,1024]{1,0:T(8,128)(2,1)S(1)} %pad_maximum_fusion.2), channel_id=1, source_target_pairs={{0,30},{1,31},{2,0},{3,1},{4,2},{5,3},{6,4},{7,5},{8,6},{9,7},{10,... | collective-permute-start | bytes 1671176 | tf_op jit(solution)/shard_map/ppermute | solution.py:12

commit v2 on v0

v2 whole, which is shorter than its diff:
```python
import functools

import jax
import jax.numpy as jnp
from jax import lax
from jax.experimental import pallas as pl
from jax.experimental.pallas import tpu as pltpu
from jax.sharding import PartitionSpec as P

PARTS = 2
EXTRA = 16
TILE = 512
LANES = 128
NORM = 256
F32 = jnp.float32
BF16 = jnp.bfloat16
VMEM = pl.BlockSpec(memory_space=pltpu.VMEM)
HBM = pl.BlockSpec(memory_space=pltpu.HBM)
SMEM = pl.BlockSpec(memory_space=pltpu.SMEM)


def shift(value, steps):
    count = lax.axis_size("blk")
    return lax.ppermute(value, "blk", [(i, (i + steps) % count) for i in range(count)])


def partner(value):
    count = lax.axis_size("blk")
    return lax.ppermute(value, "blk", [(i, i ^ 1) for i in range(count)])


def call(kernel, outs, scratch=(), specs=(), name=None, aliases=None, mib=12):
    return pl.pallas_call(
        kernel,
        out_shape=[jax.ShapeDtypeStruct(s, d) for s, d in outs],
        in_specs=list(specs),
        out_specs=[VMEM] * len(outs),
        scratch_shapes=list(scratch),
        input_output_aliases=aliases or {},
        compiler_params=pltpu.CompilerParams(vmem_limit_bytes=mib << 20),
        cost_estimate=pl.CostEstimate(flops=1000, bytes_accessed=1000, transcendentals=0),
        name=name,
    )


def column(row, rows):
    return jnp.transpose(jnp.broadcast_to(row, (LANES, rows)))


def weigh(codes, scale, points, logs, cut, weights, total):
    similarity = lax.dot_general(
        codes, points, (((1,), (1,)), ((), ())), preferred_element_type=F32
    )
    weight = jnp.exp(similarity * jnp.tile(scale, (1, TILE // LANES)) - logs[:, cut])
    weights[:, cut] = weight.astype(BF16)
    for lane in range(0, TILE, LANES):
        piece = weight[:, lane : lane + LANES]
        total = piece if total is None else total + piece
    return jnp.sum(weight, axis=0, keepdims=True), total


def row_of(total):
    return jnp.sum(jnp.transpose(total), axis=0, keepdims=True)


def tiles_of(count):
    return [slice(t * TILE, (t + 1) * TILE) for t in range(count // TILE)]


def norm_tile(raw, unit, cut):
    for start in range(cut.start, cut.stop, NORM):
        some = slice(start, start + NORM)
        wide = raw[some, :].astype(F32)
        scale = lax.rsqrt(jnp.mean(wide * wide, axis=1, keepdims=True) + 1e-06)
        unit[some, :] = (wide * scale).astype(BF16)


def block(part, codes, scales, fetch, unit, logs, weights, numer, sums, point_sum, add):
    cuts = [slice(k * part, (k + 1) * part) for k in range(codes.shape[0] // part)]
    wide = [column(scales[:, cut], part) for cut in cuts]
    totals = [None] * len(cuts)
    tiles = tiles_of(unit.shape[0])
    fetch(0)
    for t, tile in enumerate(tiles):
        points = unit[tile, :]
        if t + 1 < len(tiles):
            fetch(t + 1)
        line = 0.0
        for k, cut in enumerate(cuts):
            some, totals[k] = weigh(
                codes[cut, :], wide[k], points, logs, tile, weights.at[k], totals[k]
            )
            line = line + some
        point_sum[:, tile] = line
    for k, cut in enumerate(cuts):
        value = jnp.dot(weights[k], unit[...], preferred_element_type=F32)
        if add:
            numer[cut, :] += value
            sums[:, cut] += row_of(totals[k])
        else:
            numer[cut, :] = value
            sums[:, cut] = row_of(totals[k])


def local_kernel(
    part, odd, own_raw, other_raw, own_codes, scales, logs, other_logs,
    unit, other_unit, numer, sums, point_sum, other_sum,
    raw, codes, weights, sems, code_sem,
):
    tiles = tiles_of(unit.shape[0])

    def copies(source, at):
        return [
            pltpu.make_async_copy(source.at[tile, :], raw.at[at, tile, :], sems.at[at, t])
            for t, tile in enumerate(tiles)
        ]

    first, second = copies(own_raw, 0), copies(other_raw, 1)
    code_copy = pltpu.make_async_copy(own_codes, codes, code_sem)
    for copy in [first[0], code_copy] + first[1:] + second:
        copy.start()

    def fetch(t):
        first[t].wait()
        norm_tile(raw.at[0], unit, tiles[t])
        if t == 0:
            code_copy.wait()

    def fetch_other(t):
        second[t].wait()
        norm_tile(raw.at[1], other_unit, tiles[t])

    block(part, codes, scales, fetch, unit, logs, weights, numer, sums, point_sum, False)

    @pl.when(odd[0] == 0)
    def _():
        block(
            part, codes, scales, fetch_other, other_unit, other_logs, weights, numer, sums, other_sum, True
        )

    @pl.when(odd[0] == 1)
    def _():
        for t in range(len(tiles)):
            fetch_other(t)
        other_sum[...] = jnp.zeros_like(other_sum)


def moved_kernel(
    k, part, odd, codes, scales, points, logs, others, other_logs, sums0, point_before, other_before,
    sent, sums, point_sum, other_sum, weights, numer,
):
    rows = PARTS * part
    cut = slice(k * part, (k + 1) * part)
    scale = column(scales[part : part + EXTRA, :rows].astype(F32)[:1, cut], part)

    def weigh_all(rows, row_logs, before, after):
        total = None
        for tile in tiles_of(rows.shape[0]):
            line, total = weigh(
                codes[:part, :], scale, rows[tile, :], row_logs, tile, weights, total
            )
            after[:, tile] = before[:, tile] + line
        return row_of(total)

    sums[...] = sums0[...]
    sums[:, cut] = weigh_all(points, logs, point_before, point_sum)

    @pl.when(odd[0] == 0)
    def _():
        other_sum[...] = other_before[...]
        value = jnp.dot(weights[...], points[...], preferred_element_type=F32)
        sent[:part, :] = value.astype(BF16)

    @pl.when(odd[0] == 1)
    def _():
        numer[...] = jnp.dot(weights[...], points[...], preferred_element_type=F32)
        sums[:, cut] += weigh_all(others, other_logs, other_before, other_sum)
        value = numer[...] + jnp.dot(weights[...], others[...], preferred_element_type=F32)
        sent[:part, :] = value.astype(BF16)

    if sent.shape[0] > part:
        high = sums[...].astype(BF16).astype(F32)
        row = lax.broadcasted_iota(jnp.int32, (EXTRA, rows), 0)
        ends = jnp.where(row == 0, high, jnp.where(row == 1, sums[...] - high, 0.0))
        sent[part:, :] = jnp.zeros((EXTRA, sent.shape[1]), BF16)
        sent[part:, :rows] = ends.astype(BF16)


def last_kernel(k, part, numer, back, sums, *refs):
    *refs, out, mass = refs if back.shape[0] > part else (*refs, None)
    rows = out.shape[0]
    start = pl.multiple_of(pl.program_id(0) * rows, rows)
    total = numer[pl.ds(k * part + start, rows), :] + back[pl.ds(start, rows), :].astype(F32)
    out[...] = total * lax.rsqrt(jnp.mean(total * total, axis=1, keepdims=True) + 1e-06)
    if mass is not None:
        ends = back[part:, : mass.shape[1]].astype(F32)
        mass[...] = jnp.log(sums[...] + jnp.sum(ends, axis=0, keepdims=True))


def last(k, part, numer, back, sums, before):
    width = back.shape[1]
    steps = 2
    more = [] if before is None else [before]
    outs = [numer, sums] if back.shape[0] > part else [numer]
    return pl.pallas_call(
        functools.partial(last_kernel, k, part),
        grid=(steps,),
        out_shape=[jax.ShapeDtypeStruct(out.shape, F32) for out in outs],
        in_specs=[VMEM, VMEM, VMEM] + [HBM] * len(more),
        out_specs=[pl.BlockSpec((part // steps, width), lambda i: (k * steps + i, 0)), VMEM][: len(outs)],
        input_output_aliases={3: 0} if more else {},
        compiler_params=pltpu.CompilerParams(vmem_limit_bytes=6 << 20),
        cost_estimate=pl.CostEstimate(flops=1000, bytes_accessed=1000, transcendentals=0),
        name=f"last{k}",
    )(numer, back, sums, *more)


def on_device(embeddings, centroid_codes, centroid_scales, log_normalizers):
    odd = (lax.axis_index("blk") & 1).astype(jnp.int32).reshape(1)
    rows, width = centroid_codes.shape
    points = embeddings.shape[0]
    part = rows // PARTS
    cuts = [slice(k * part, (k + 1) * part) for k in range(PARTS)]
    scale_rows = jnp.pad(centroid_scales.reshape(1, rows), ((0, EXTRA - 1), (0, width - rows)))
    received = [shift(jnp.concatenate([centroid_codes[cuts[0]], scale_rows], axis=0), 2)]
    received += [shift(lax.optimization_barrier(centroid_codes)[cut], 2) for cut in cuts[1:]]
    scales = centroid_scales.astype(F32).reshape(1, rows)
    logs = log_normalizers.astype(F32).reshape(1, points)
    other_raw = partner(embeddings)
    other_logs = partner(log_normalizers).astype(F32).reshape(1, points)
    line = ((1, points), F32)
    units = ((points, width), BF16)
    unit_rows, other_rows, numer, own_sum, point_total, other_total = call(
        functools.partial(local_kernel, part),
        [units, units, ((rows, width), F32), ((1, rows), F32), line, line],
        [
            pltpu.VMEM((2, points, width), BF16),
            pltpu.VMEM((rows, width), BF16),
            pltpu.VMEM((PARTS, part, points), BF16),
            pltpu.SemaphoreType.DMA((2, points // TILE)),
            pltpu.SemaphoreType.DMA(()),
        ],
        [SMEM, HBM, HBM, HBM] + [VMEM] * 3,
        "local",
        mib=24,
    )(odd, embeddings, other_raw, centroid_codes, scales, logs, other_logs)
    back = []
    sums = jnp.zeros((1, rows), F32)
    for k in range(PARTS):
        more = EXTRA if k == PARTS - 1 else 0
        sent, sums, point_total, other_total = call(
            functools.partial(moved_kernel, k, part),
            [((part + more, width), BF16), ((1, rows), F32), line, line],
            [pltpu.VMEM((part, points), BF16), pltpu.VMEM((part, width), F32)],
            [SMEM] + [VMEM] * 9,
            f"moved{k}",
        )(
            odd, received[k], received[0], unit_rows, logs, other_rows, other_logs, sums,
            point_total, other_total,
        )
        back.append(shift(sent, -2))
    back[0], other_total = lax.optimization_barrier((back[0], other_total))
    point_mass = jnp.log(point_total + partner(other_total))
    back[-1], point_mass = lax.optimization_barrier((back[-1], point_mass))
    new_centroids = None
    for k in range(PARTS):
        new_centroids, *mass_log = last(k, part, numer, back[k], own_sum, new_centroids)
    return (new_centroids, mass_log[0].reshape(rows), point_mass.reshape(points))


def solution(mesh):
    return jax.shard_map(
        on_device,
        mesh=mesh,
        in_specs=(P("blk", None), P("blk", None), P("blk"), P("blk")),
        out_specs=(P("blk", None), P("blk"), P("blk")),
        check_vma=False,
    )
```

time: 151 us -> 56.3 us (0.37)
  waiting for transfers between devices: 86.9 us -> 14.4 us
  starting transfers between devices: 37.8 us -> 13.8 us
  Pallas kernels: 0 us -> 22.5 us
  matrix products: 18.1 us -> 0 us
  other arithmetic: 6.01 us -> 0.66 us
  local copies, waits for them, and re-layouts: 0.77 us -> 4 us
    ppermute x10 -> x7, waiting for transfers between devices: 86.9 us -> 14.4 us  [the longest x4 13.5 us: shift(): lax.ppermute(value, 'blk', [(i, (i + steps) % count) for i in range(count)])]
    ppermute x10 -> x7, starting transfers between devices: 37.8 us -> 13.8 us  [the longest x4 13.1 us: shift(): lax.ppermute(value, 'blk', [(i, (i + steps) % count) for i in range(count)])]
    pallas_call x0 -> x5, Pallas kernels: none -> 22.5 us  [the longest x1 13.9 us: on_device(): call(functools.partial(local_kernel, part), [units, units, ((rows, width)...]
    dot_general x6 -> x0, matrix products: 18.1 us -> none  [the longest x3 10.7 us: weigh(): similarity = jnp.dot(unit_rows, codes.T, preferred_element_type=jnp.float32)]
    reduce_sum x2 -> x0, other arithmetic: 3.44 us -> none  [the longest x1 3.22 us: on_device(): jnp.mean(wide_points * wide_points, axis=1, keepdims=True) + 1e-06]
    unnamed x8, local copies, waits for them, and re-layouts: 0.18 us -> 2.2 us
    mul x1 -> x0, other arithmetic: 1.53 us -> none  [on_device(): numerator * lax.rsqrt(jnp.mean(numerator * numerator, axis=1, keepdims=Tr...]
  transfers between devices with their start and end apart: 10 -> 7, of which waited for: 5 -> 4; matrix products, arithmetic and copies ran while one was open for 8% -> 4% of each run, Pallas kernels for 0% -> 38%
where the time goes in v2:
time: 56.3 us; the launch traced here: 56.1 us
  Pallas kernels  22.5 us (40%)
  waiting for transfers between devices  14.4 us (26%)
  starting transfers between devices  13.8 us (25%)
  local copies, waits for them, and re-layouts  4 us (7%)
  between operations  0.72 us (1%)
  other arithmetic  0.66 us (1%)
    pallas_call x1, Pallas kernels, on_device(): call(functools.partial(local_kernel, part), [units, units, ((rows, width)...  13.9 us
    ppermute x4, waiting for transfers between devices, shift(): lax.ppermute(value, 'blk', [(i, (i + steps) % count) for i in range(count)])  13.5 us
    ppermute x4, starting transfers between devices, shift(): lax.ppermute(value, 'blk', [(i, (i + steps) % count) for i in range(count)])  13.1 us
    pallas_call x2, Pallas kernels, on_device(): call(functools.partial(moved_kernel, k, part), [((part + more, width), BF...  6.33 us
    pallas_call x2, Pallas kernels, last(): pl.pallas_call(functools.partial(last_kernel, k, part), grid=(steps,), ou...  2.28 us
    unnamed x8, local copies, waits for them, and re-layouts  2.2 us
  transfers between devices with their start and end apart: 7, of which 4 were waited for; matrix products, arithmetic and copies ran while one was open for 4% of the time, Pallas kernels for 38%

profile of v2, /device:TPU:0, one launch (start us, length us, event | category | flops | bytes accessed | tf_op | source)
XLA Modules:
  0.0 56.1 jit_solution(15186918746520898698)
XLA Ops:
  0.6 0.0 copy-start.1
  0.6 0.0 copy-start.3
  0.7 0.0 copy-start.2
  0.7 0.5 collective-permute-start
  1.2 1.1 %slice.7 = bf16[256,1024]{1,0:T(8,128)(2,1)S(1)} slice(bf16[512,1024]{1,0:T(8,128)(2,1)} %own_codes.1), slice={[0:256], [0:1024]} | slice | bytes 1048576 | tf_op jit(solution)/shard_map/slice | solution.py:225
  2.3 0.7 %reshape.32 = bf16[1,512]{1,0:T(2,128)(2,1)S(1)} reshape(bf16[512]{0:T(512)(128)(2,1)} %param.6) | data formatting | bytes 2048 | tf_op jit(solution)/shard_map/reshape | solution.py:227
  3.0 2.6 %collective-permute-start.3 = (bf16[272,1024]{1,0:T(8,128)(2,1)S(1)}, bf16[272,1024]{1,0:T(8,128)(2,1)S(1)}, u32[]{:S(2)}, u32[]{:S(2)}) collective-permute-start(bf16[272,1024]{1,0:T(8,128)(2,1)S(1)} %fusion.1), channel_id=1, source_target_pairs={{0,2},{1,3},{2,4},{3,5},{4,6},{5,7},{6,8},{7,9},{8,10},{9,11},{10,... | collective-permute-start | bytes 1671176 | tf_op jit(solution)/shard_map/ppermute | solution.py:24
  5.6 0.0 copy-done.2
  5.6 0.2 collective-permute-start.1
  5.8 0.0 copy-done.1
  5.8 1.5 %collective-permute-start.2 = (bf16[256,1024]{1,0:T(8,128)(2,1)S(1)}, bf16[256,1024]{1,0:T(8,128)(2,1)S(1)}, u32[]{:S(2)}, u32[]{:S(2)}) collective-permute-start(bf16[256,1024]{1,0:T(8,128)(2,1)S(1)} %slice.8), channel_id=1, source_target_pairs={{0,2},{1,3},{2,4},{3,5},{4,6},{5,7},{6,8},{7,9},{8,10},{9,11},{10,... | collective-permute-start | bytes 1572872 | tf_op jit(solution)/shard_map/ppermute | solution.py:24
  7.4 0.0 copy-done.3
  7.4 0.6 %collective-permute-done.1 = bf16[2048]{0:T(1024)(128)(2,1)S(1)} collective-permute-done((bf16[2048]{0:T(1024)(128)(2,1)S(1)}, bf16[2048]{0:T(1024)(128)(2,1)S(1)}, u32[]{:S(2)}, u32[]{:S(2)}) %collective-permute-start.1) | collective-permute-done | bytes 4128 | tf_op jit(solution)/shard_map/ppermute | solution.py:29
  8.0 0.3 collective-permute-done.other_raw
  8.3 0.0 copy-start
  8.3 2.2 %copy-done = bf16[2048,1024]{1,0:T(8,128)(2,1)S(1)} copy-done((bf16[2048,1024]{1,0:T(8,128)(2,1)S(1)}, bf16[2048,1024]{1,0:T(8,128)(2,1)}, u32[]{:S(2)}) %copy-start) | copy-done | bytes 4194328
  10.5 13.9 %local.1 = (bf16[2048,1024]{1,0:T(8,128)(2,1)S(1)}, bf16[2048,1024]{1,0:T(8,128)(2,1)S(1)}, f32[512,1024]{1,0:T(8,128)S(1)}, f32[1,512]{1,0:T(1,128)S(1)}, f32[1,2048]{1,0:T(1,128)S(1)}, /*index=5*/f32[1,2048]{1,0:T(1,128)S(1)}) custom-call(s32[1]{0:T(128)} %bitcast.odd, bf16[2048,1024]{1,0:T(8,128)(2,1)S(1)} %copy-done, ...), custom_call_target="tpu_custom_call" | custom-call | flops 1000 | bytes 1000 | tf_op jit(solution)/shard_map/local/pallas_call | solution.py:233
  24.4 0.0 collective-permute-done.3.codes.scales
  24.5 2.9 %moved0.1 = (bf16[256,1024]{1,0:T(8,128)(2,1)S(1)}, f32[1,512]{1,0:T(1,128)S(1)}, f32[1,2048]{1,0:T(1,128)S(1)}, f32[1,2048]{1,0:T(1,128)S(1)}) custom-call(s32[1]{0:T(128)} %bitcast.odd, bf16[272,1024]{1,0:T(8,128)(2,1)S(1)} %collective-permute-done.3.codes.scales, bf16[272,1024]{1,0:T(8,128)(2,1)S(1)} %collective-permute-done.3.codes.scales, ...), custom_call_target="tpu_custom_call" | custom-call | flops 1000 | bytes 1000 | tf_op jit(solution)/shard_map/moved0/pallas_call | solution.py:251
  27.3 7.1 %collective-permute-start.5 = (bf16[256,1024]{1,0:T(8,128)(2,1)S(1)}, bf16[256,1024]{1,0:T(8,128)(2,1)S(1)}, u32[]{:S(2)}, u32[]{:S(2)}) collective-permute-start(bf16[256,1024]{1,0:T(8,128)(2,1)S(1)} %get-tuple-element.32), channel_id=1, source_target_pairs={{0,30},{1,31},{2,0},{3,1},{4,2},{5,3},{6,4},{7,5},{8,6},{9,7},{10,... | collective-permute-start | bytes 1572872 | tf_op jit(solution)/shard_map/ppermute | solution.py:24
  34.5 0.0 collective-permute-done.2.codes
  34.5 3.5 %moved1.1 = (bf16[272,1024]{1,0:T(8,128)(2,1)S(1)}, f32[1,512]{1,0:T(1,128)}, f32[1,2048]{1,0:T(1,128)S(1)}, f32[1,2048]{1,0:T(1,128)S(1)}) custom-call(s32[1]{0:T(128)} %bitcast.odd, bf16[256,1024]{1,0:T(8,128)(2,1)S(1)} %collective-permute-done.2.codes, bf16[272,1024]{1,0:T(8,128)(2,1)S(1)} %collective-permute-done.3.codes.scales, ...), custom_call_target="tpu_custom_call" | custom-call | flops 1000 | bytes 1000 | tf_op jit(solution)/shard_map/moved1/pallas_call | solution.py:251
  37.9 1.8 %collective-permute-start.4 = (bf16[272,1024]{1,0:T(8,128)(2,1)S(1)}, bf16[272,1024]{1,0:T(8,128)(2,1)S(1)}, u32[]{:S(2)}, u32[]{:S(2)}) collective-permute-start(bf16[272,1024]{1,0:T(8,128)(2,1)S(1)} %get-tuple-element.30), channel_id=1, source_target_pairs={{0,30},{1,31},{2,0},{3,1},{4,2},{5,3},{6,4},{7,5},{8,6},{9,7},{10,... | collective-permute-start | bytes 1671176 | tf_op jit(solution)/shard_map/ppermute | solution.py:24
  39.7 4.8 %collective-permute-done.5.back = bf16[256,1024]{1,0:T(8,128)(2,1)S(1)} collective-permute-done((bf16[256,1024]{1,0:T(8,128)(2,1)S(1)}, bf16[256,1024]{1,0:T(8,128)(2,1)S(1)}, u32[]{:S(2)}, u32[]{:S(2)}) %collective-permute-start.5) | collective-permute-done | bytes 524320 | tf_op jit(solution)/shard_map/ppermute | solution.py:24
  44.5 0.0 collective-permute-start.6
  44.5 1.1 %last0.1.refs_0_ = f32[512,1024]{1,0:T(8,128)} custom-call(f32[512,1024]{1,0:T(8,128)S(1)} %get-tuple-element.22.numer, bf16[256,1024]{1,0:T(8,128)(2,1)S(1)} %collective-permute-done.5.back, f32[1,512]{1,0:T(1,128)S(1)} %get-tuple-element.36.sums), custom_call_target="tpu_custom_call" | custom-call | flops 1000 | bytes 1000 | tf_op jit(solution)/shard_map/last0/pallas_call | solution.py:205
  45.6 0.0 collective-permute-done.6
  45.7 0.6 %add_log_fusion = f32[1,2048]{1,0:T(1,128)} fusion(f32[1,2048]{1,0:T(1,128)S(1)} %get-tuple-element.31, f32[1,2048]{1,0:T(1,128)S(1)} %collective-permute-done.6), kind=kLoop, calls=%fused_computation.3 | loop fusion | flops 2048 | bytes 24576 | tf_op jit(solution)/shard_map/log | solution.py:263
  46.3 8.7 %collective-permute-done.4.back = bf16[272,1024]{1,0:T(8,128)(2,1)S(1)} collective-permute-done((bf16[272,1024]{1,0:T(8,128)(2,1)S(1)}, bf16[272,1024]{1,0:T(8,128)(2,1)S(1)}, u32[]{:S(2)}, u32[]{:S(2)}) %collective-permute-start.4) | collective-permute-done | bytes 557088 | tf_op jit(solution)/shard_map/ppermute | solution.py:24
  55.0 1.1 %last1.1 = (f32[512,1024]{1,0:T(8,128)}, f32[1,512]{1,0:T(1,128)}) custom-call(f32[512,1024]{1,0:T(8,128)S(1)} %get-tuple-element.22.numer, bf16[272,1024]{1,0:T(8,128)(2,1)S(1)} %collective-permute-done.4.back, f32[1,512]{1,0:T(1,128)S(1)} %get-tuple-element.36.sums, f32[512,1024]{1,0:T(8,128)} %last0.1.refs_0_), custom_call_target="tpu_custom_call", output_to_operand_aliasing={{0}: (3, {})} | custom-call | flops 1000 | bytes 1000 | tf_op jit(solution)/shard_map/last1/pallas_call | solution.py:205
  (6 shorter events, 0.1 us)
Async XLA Ops:
  0.6 5.1 %copy-start.1 = (bf16[512,1024]{1,0:T(8,128)(2,1)S(1)}, bf16[512,1024]{1,0:T(8,128)(2,1)}, u32[]{:S(2)}) copy-start(bf16[512,1024]{1,0:T(8,128)(2,1)} %own_codes.1) | copy-start | bytes 3145732
  0.6 6.7 %copy-start.3 = (bf16[512]{0:T(512)(128)(2,1)S(1)}, bf16[512]{0:T(512)(128)(2,1)}, u32[]{:S(2)}) copy-start(bf16[512]{0:T(512)(128)(2,1)} %param.6) | copy-start | bytes 3076
  0.7 5.0 %copy-start.2 = (bf16[2048]{0:T(1024)(128)(2,1)S(1)}, bf16[2048]{0:T(1024)(128)(2,1)}, u32[]{:S(2)}) copy-start(bf16[2048]{0:T(1024)(128)(2,1)} %param.7) | copy-start | bytes 12292
  0.7 7.6 %collective-permute-start = (bf16[2048,1024]{1,0:T(8,128)(2,1)}, bf16[2048,1024]{1,0:T(8,128)(2,1)}, u32[]{:S(2)}, u32[]{:S(2)}) collective-permute-start(bf16[2048,1024]{1,0:T(8,128)(2,1)} %own_raw.1), channel_id=1, source_target_pairs={{0,1},{1,0},{2,3},{3,2},{4,5},{5,4},{6,7},{7,6},{8,9},{9,8},{10,11... | collective-permute-start | bytes 12582920 | tf_op jit(solution)/shard_map/ppermute | solution.py:29
  3.0 21.5 %collective-permute-start.3 = (bf16[272,1024]{1,0:T(8,128)(2,1)S(1)}, bf16[272,1024]{1,0:T(8,128)(2,1)S(1)}, u32[]{:S(2)}, u32[]{:S(2)}) collective-permute-start(bf16[272,1024]{1,0:T(8,128)(2,1)S(1)} %fusion.1), channel_id=1, source_target_pairs={{0,2},{1,3},{2,4},{3,5},{4,6},{5,7},{6,8},{7,9},{8,10},{9,11},{10,... | collective-permute-start | bytes 1671176 | tf_op jit(solution)/shard_map/ppermute | solution.py:24
  5.6 2.4 %collective-permute-start.1 = (bf16[2048]{0:T(1024)(128)(2,1)S(1)}, bf16[2048]{0:T(1024)(128)(2,1)S(1)}, u32[]{:S(2)}, u32[]{:S(2)}) collective-permute-start(bf16[2048]{0:T(1024)(128)(2,1)S(1)} %copy-done.2), channel_id=1, source_target_pairs={{0,1},{1,0},{2,3},{3,2},{4,5},{5,4},{6,7},{7,6},{8,9},{9,8},{10,11... | collective-permute-start | bytes 12296 | tf_op jit(solution)/shard_map/ppermute | solution.py:29
  5.8 28.6 %collective-permute-start.2 = (bf16[256,1024]{1,0:T(8,128)(2,1)S(1)}, bf16[256,1024]{1,0:T(8,128)(2,1)S(1)}, u32[]{:S(2)}, u32[]{:S(2)}) collective-permute-start(bf16[256,1024]{1,0:T(8,128)(2,1)S(1)} %slice.8), channel_id=1, source_target_pairs={{0,2},{1,3},{2,4},{3,5},{4,6},{5,7},{6,8},{7,9},{8,10},{9,11},{10,... | collective-permute-start | bytes 1572872 | tf_op jit(solution)/shard_map/ppermute | solution.py:24
  8.3 2.2 %copy-start = (bf16[2048,1024]{1,0:T(8,128)(2,1)S(1)}, bf16[2048,1024]{1,0:T(8,128)(2,1)}, u32[]{:S(2)}) copy-start(bf16[2048,1024]{1,0:T(8,128)(2,1)} %own_raw.1) | copy-start | bytes 12582916
  27.3 17.1 %collective-permute-start.5 = (bf16[256,1024]{1,0:T(8,128)(2,1)S(1)}, bf16[256,1024]{1,0:T(8,128)(2,1)S(1)}, u32[]{:S(2)}, u32[]{:S(2)}) collective-permute-start(bf16[256,1024]{1,0:T(8,128)(2,1)S(1)} %get-tuple-element.32), channel_id=1, source_target_pairs={{0,30},{1,31},{2,0},{3,1},{4,2},{5,3},{6,4},{7,5},{8,6},{9,7},{10,... | collective-permute-start | bytes 1572872 | tf_op jit(solution)/shard_map/ppermute | solution.py:24
  37.9 17.1 %collective-permute-start.4 = (bf16[272,1024]{1,0:T(8,128)(2,1)S(1)}, bf16[272,1024]{1,0:T(8,128)(2,1)S(1)}, u32[]{:S(2)}, u32[]{:S(2)}) collective-permute-start(bf16[272,1024]{1,0:T(8,128)(2,1)S(1)} %get-tuple-element.30), channel_id=1, source_target_pairs={{0,30},{1,31},{2,0},{3,1},{4,2},{5,3},{6,4},{7,5},{8,6},{9,7},{10,... | collective-permute-start | bytes 1671176 | tf_op jit(solution)/shard_map/ppermute | solution.py:24
  44.5 1.2 %collective-permute-start.6 = (f32[1,2048]{1,0:T(1,128)S(1)}, f32[1,2048]{1,0:T(1,128)S(1)}, u32[]{:S(2)}, u32[]{:S(2)}) collective-permute-start(f32[1,2048]{1,0:T(1,128)S(1)} %get-tuple-element.34), channel_id=1, source_target_pairs={{0,1},{1,0},{2,3},{3,2},{4,5},{5,4},{6,7},{7,6},{8,9},{9,8},{10,11... | collective-permute-start | bytes 24584 | tf_op jit(solution)/shard_map/ppermute | solution.py:29

commit v3 on v2

--- a/solution.py
+++ b/solution.py
@@ -7,7 +7,8 @@
 from jax.experimental.pallas import tpu as pltpu
 from jax.sharding import PartitionSpec as P
 
-PARTS = 2
+HALVES = 2
+SIZES = (256, 256)
 EXTRA = 16
 TILE = 512
 LANES = 128
@@ -146,12 +147,12 @@
 
 
 def moved_kernel(
-    k, part, odd, codes, scales, points, logs, others, other_logs, sums0, point_before, other_before,
+    cut, odd, codes, scales, points, logs, others, other_logs, sums0, point_before, other_before,
     sent, sums, point_sum, other_sum, weights, numer,
 ):
-    rows = PARTS * part
-    cut = slice(k * part, (k + 1) * part)
-    scale = column(scales[part : part + EXTRA, :rows].astype(F32)[:1, cut], part)
+    part, rows = cut.stop - cut.start, sums0.shape[1]
+    first = scales.shape[0] - EXTRA
+    scale = column(scales[first:, :rows].astype(F32)[:1, cut], part)
 
     def weigh_all(rows, row_logs, before, after):
         total = None
@@ -178,51 +179,56 @@
         value = numer[...] + jnp.dot(weights[...], others[...], preferred_element_type=F32)
         sent[:part, :] = value.astype(BF16)
 
-    if sent.shape[0] > part:
-        high = sums[...].astype(BF16).astype(F32)
-        row = lax.broadcasted_iota(jnp.int32, (EXTRA, rows), 0)
-        ends = jnp.where(row == 0, high, jnp.where(row == 1, sums[...] - high, 0.0))
-        sent[part:, :] = jnp.zeros((EXTRA, sent.shape[1]), BF16)
-        sent[part:, :rows] = ends.astype(BF16)
-
-
-def last_kernel(k, part, numer, back, sums, *refs):
-    *refs, out, mass = refs if back.shape[0] > part else (*refs, None)
+
+def first_rows(cut, numer, back, out):
     rows = out.shape[0]
     start = pl.multiple_of(pl.program_id(0) * rows, rows)
-    total = numer[pl.ds(k * part + start, rows), :] + back[pl.ds(start, rows), :].astype(F32)
+    total = numer[pl.ds(cut.start + start, rows), :] + back[pl.ds(start, rows), :].astype(F32)
     out[...] = total * lax.rsqrt(jnp.mean(total * total, axis=1, keepdims=True) + 1e-06)
-    if mass is not None:
-        ends = back[part:, : mass.shape[1]].astype(F32)
-        mass[...] = jnp.log(sums[...] + jnp.sum(ends, axis=0, keepdims=True))
-
-
-def last(k, part, numer, back, sums, before):
-    width = back.shape[1]
+
+
+def last_rows(cut, numer, back, sums, back_sums, before, out, mass):
+    del before
+    first_rows(cut, numer, back, out)
+    mass[...] = jnp.log(sums[...] + back_sums[...])
+
+
+def finish(cut, numer, back, *more):
+    part, width = back.shape
     steps = 2
-    more = [] if before is None else [before]
-    outs = [numer, sums] if back.shape[0] > part else [numer]
+    block = part // steps
+    shapes = [jax.ShapeDtypeStruct(numer.shape, F32)]
+    specs = [pl.BlockSpec((block, width), lambda i: (cut.start // block + i, 0))]
+    if more:
+        shapes.append(jax.ShapeDtypeStruct(more[0].shape, F32))
+        specs.append(VMEM)
     return pl.pallas_call(
-        functools.partial(last_kernel, k, part),
+        functools.partial(last_rows if more else first_rows, cut),
         grid=(steps,),
-        out_shape=[jax.ShapeDtypeStruct(out.shape, F32) for out in outs],
-        in_specs=[VMEM, VMEM, VMEM] + [HBM] * len(more),
-        out_specs=[pl.BlockSpec((part // steps, width), lambda i: (k * steps + i, 0)), VMEM][: len(outs)],
-        input_output_aliases={3: 0} if more else {},
+        out_shape=shapes,
+        in_specs=[VMEM, VMEM] + ([VMEM, VMEM, HBM] if more else []),
+        out_specs=specs,
+        input_output_aliases={4: 0} if more else {},
         compiler_params=pltpu.CompilerParams(vmem_limit_bytes=6 << 20),
         cost_estimate=pl.CostEstimate(flops=1000, bytes_accessed=1000, transcendentals=0),
-        name=f"last{k}",
-    )(numer, back, sums, *more)
+        name=f"finish{cut.start}",
+    )(numer, back, *more)
 
 
 def on_device(embeddings, centroid_codes, centroid_scales, log_normalizers):
     odd = (lax.axis_index("blk") & 1).astype(jnp.int32).reshape(1)
     rows, width = centroid_codes.shape
     points = embeddings.shape[0]
-    part = rows // PARTS
-    cuts = [slice(k * part, (k + 1) * part) for k in range(PARTS)]
-    scale_rows = jnp.pad(centroid_scales.reshape(1, rows), ((0, EXTRA - 1), (0, width - rows)))
-    received = [shift(jnp.concatenate([centroid_codes[cuts[0]], scale_rows], axis=0), 2)]
+    half = rows // HALVES
+    ends = [sum(SIZES[: k + 1]) for k in range(len(SIZES))]
+    cuts = [slice(end - size, end) for end, size in zip(ends, SIZES)]
+    assert ends[-1] == rows
+    row = lax.broadcasted_iota(jnp.int32, (cuts[0].stop + EXTRA, rows), 0)
+    first = centroid_codes[: cuts[0].stop + EXTRA]
+    first = jnp.concatenate(
+        [jnp.where(row < cuts[0].stop, first[:, :rows], centroid_scales), first[:, rows:]], axis=1
+    )
+    received = [shift(first, 2)]
     received += [shift(lax.optimization_barrier(centroid_codes)[cut], 2) for cut in cuts[1:]]
     scales = centroid_scales.astype(F32).reshape(1, rows)
     logs = log_normalizers.astype(F32).reshape(1, points)
@@ -231,12 +237,12 @@
     line = ((1, points), F32)
     units = ((points, width), BF16)
     unit_rows, other_rows, numer, own_sum, point_total, other_total = call(
-        functools.partial(local_kernel, part),
+        functools.partial(local_kernel, half),
         [units, units, ((rows, width), F32), ((1, rows), F32), line, line],
         [
             pltpu.VMEM((2, points, width), BF16),
             pltpu.VMEM((rows, width), BF16),
-            pltpu.VMEM((PARTS, part, points), BF16),
+            pltpu.VMEM((HALVES, half, points), BF16),
             pltpu.SemaphoreType.DMA((2, points // TILE)),
             pltpu.SemaphoreType.DMA(()),
         ],
@@ -246,11 +252,11 @@
     )(odd, embeddings, other_raw, centroid_codes, scales, logs, other_logs)
     back = []
     sums = jnp.zeros((1, rows), F32)
-    for k in range(PARTS):
-        more = EXTRA if k == PARTS - 1 else 0
+    for k, cut in enumerate(cuts):
+        part = cut.stop - cut.start
         sent, sums, point_total, other_total = call(
-            functools.partial(moved_kernel, k, part),
-            [((part + more, width), BF16), ((1, rows), F32), line, line],
+            functools.partial(moved_kernel, cut),
+            [((part, width), BF16), ((1, rows), F32), line, line],
             [pltpu.VMEM((part, points), BF16), pltpu.VMEM((part, width), F32)],
             [SMEM] + [VMEM] * 9,
             f"moved{k}",
@@ -259,13 +265,13 @@
             point_total, other_total,
         )
         back.append(shift(sent, -2))
-    back[0], other_total = lax.optimization_barrier((back[0], other_total))
+    *back[:-1], other_total, sums = lax.optimization_barrier((*back[:-1], other_total, sums))
     point_mass = jnp.log(point_total + partner(other_total))
-    back[-1], point_mass = lax.optimization_barrier((back[-1], point_mass))
-    new_centroids = None
-    for k in range(PARTS):
-        new_centroids, *mass_log = last(k, part, numer, back[k], own_sum, new_centroids)
-    return (new_centroids, mass_log[0].reshape(rows), point_mass.reshape(points))
+    back_sums = shift(sums, -2)
+    (new_centroids,) = finish(cuts[0], numer, back[0])
+    back[1], point_mass = lax.optimization_barrier((back[1], point_mass))
+    new_centroids, mass_log = finish(cuts[1], numer, back[1], own_sum, back_sums, new_centroids)
+    return (new_centroids, mass_log.reshape(rows), point_mass.reshape(points))
 
 
 def solution(mesh):

time: 56.3 us -> 55.7 us (0.989)
  starting transfers between devices: 13.8 us -> 19.2 us
  waiting for transfers between devices: 14.4 us -> 9.54 us
  local copies, waits for them, and re-layouts: 4 us -> 2.24 us
  other arithmetic: 0.66 us -> 1.83 us
  Pallas kernels: 22.5 us -> 21.9 us
    ppermute x4 -> x5, waiting for transfers between devices: 13.5 us -> 7.89 us  [shift(): lax.ppermute(value, 'blk', [(i, (i + steps) % count) for i in range(count)])]
    ppermute x4 -> x5, starting transfers between devices: 13.1 us -> 18.7 us  [shift(): lax.ppermute(value, 'blk', [(i, (i + steps) % count) for i in range(count)])]
    select_n x0 -> x1, other arithmetic: none -> 1.14 us  [on_device(): jnp.where(row < cuts[0].stop, first[:, :rows], centroid_scales)]
    slice x1 -> x0, local copies, waits for them, and re-layouts: 1.08 us -> none  [on_device(): centroid_codes[cuts[0]]]
    reshape x1 -> x0, local copies, waits for them, and re-layouts: 0.68 us -> none  [on_device(): scales = centroid_scales.astype(F32).reshape(1, rows)]
    ppermute x3, waiting for transfers between devices: 0.96 us -> 1.65 us  [partner(): return lax.ppermute(value, 'blk', [(i, i ^ 1) for i in range(count)])]
    pallas_call x5, Pallas kernels: 22.5 us -> 21.9 us  [the longest x1 13.9 us: on_device(): call(functools.partial(local_kernel, half), [units, units, ((rows, width)...]
  transfers between devices with their start and end apart: 7 -> 8, of which waited for: 4 -> 4; matrix products, arithmetic and copies ran while one was open for 4% -> 3% of each run, Pallas kernels for 38% -> 37%
where the time goes in v3:
time: 55.7 us; the launch traced here: 55.5 us
  Pallas kernels  21.9 us (39%)
  starting transfers between devices  19.2 us (34%)
  waiting for transfers between devices  9.54 us (17%)
  local copies, waits for them, and re-layouts  2.24 us (4%)
  other arithmetic  1.83 us (3%)
  between operations  0.75 us (1%)
    ppermute x5, starting transfers between devices, shift(): lax.ppermute(value, 'blk', [(i, (i + steps) % count) for i in range(count)])  18.7 us
    pallas_call x1, Pallas kernels, on_device(): call(functools.partial(local_kernel, half), [units, units, ((rows, width)...  13.9 us
    ppermute x5, waiting for transfers between devices, shift(): lax.ppermute(value, 'blk', [(i, (i + steps) % count) for i in range(count)])  7.89 us
    pallas_call x2, Pallas kernels, on_device(): call(functools.partial(moved_kernel, cut), [((part, width), BF16), ((1, r...  5.73 us
    pallas_call x2, Pallas kernels, finish(): pl.pallas_call(functools.partial(last_rows if more else first_rows, cut),...  2.27 us
    unnamed x8, local copies, waits for them, and re-layouts  2.2 us
    ppermute x3, waiting for transfers between devices, partner(): return lax.ppermute(value, 'blk', [(i, i ^ 1) for i in range(count)])  1.65 us
    select_n x1, other arithmetic, on_device(): jnp.where(row < cuts[0].stop, first[:, :rows], centroid_scales)  1.14 us
  transfers between devices with their start and end apart: 8, of which 4 were waited for; matrix products, arithmetic and copies ran while one was open for 3% of the time, Pallas kernels for 37%

profile of v3, /device:TPU:0, one launch (start us, length us, event | category | flops | bytes accessed | tf_op | source)
XLA Modules:
  0.0 55.5 jit_solution(8842094122025104317)
XLA Ops:
  0.6 0.0 copy-start.2
  0.6 0.0 copy-start
  0.7 0.0 copy-start.3
  0.7 0.5 collective-permute-start
  1.2 1.1 %slice_select_fusion = (bf16[272,512]{1,0:T(8,128)(2,1)S(1)}, bf16[272,512]{1,0:T(8,128)(2,1)S(1)}) fusion(bf16[512,1024]{1,0:T(8,128)(2,1)} %own_codes.1, pred[272]{0:T(512)(128)(4,1)S(1)} %iota_compare_fusion, bf16[512]{0:T(512)(128)(2,1)} %param.6), kind=kLoop, calls=%fused_computation.1 | loop fusion | flops 139264 | bytes 1115408 | tf_op jit(solution)/shard_map/jit(_where)/select_n | solution.py:229
  2.3 0.1 pad_maximum_fusion
  2.4 2.6 %collective-permute-start.3 = (bf16[272,1024]{1,0:T(8,128)(2,1)S(1)}, bf16[272,1024]{1,0:T(8,128)(2,1)S(1)}, u32[]{:S(2)}, u32[]{:S(2)}) collective-permute-start(bf16[272,1024]{1,0:T(8,128)(2,1)S(1)} %pad_maximum_fusion), channel_id=1, source_target_pairs={{0,2},{1,3},{2,4},{3,5},{4,6},{5,7},{6,8},{7,9},{8,10},{9,11},{10,... | collective-permute-start | bytes 1671176 | tf_op jit(solution)/shard_map/ppermute | solution.py:25
  5.0 0.0 copy-done
  5.1 1.5 %collective-permute-start.2 = (bf16[256,1024]{1,0:T(8,128)(2,1)S(1)}, bf16[256,1024]{1,0:T(8,128)(2,1)S(1)}, u32[]{:S(2)}, u32[]{:S(2)}) collective-permute-start(bf16[256,1024]{1,0:T(8,128)(2,1)S(1)} %slice.15), channel_id=1, source_target_pairs={{0,2},{1,3},{2,4},{3,5},{4,6},{5,7},{6,8},{7,9},{8,10},{9,11},{10,... | collective-permute-start | bytes 1572872 | tf_op jit(solution)/shard_map/ppermute | solution.py:25
  6.6 0.0 copy-done.3
  6.6 0.0 collective-permute-start.1
  6.6 0.0 copy-done.2
  6.7 1.3 %collective-permute-done.1 = bf16[2048]{0:T(1024)(128)(2,1)S(1)} collective-permute-done((bf16[2048]{0:T(1024)(128)(2,1)S(1)}, bf16[2048]{0:T(1024)(128)(2,1)S(1)}, u32[]{:S(2)}, u32[]{:S(2)}) %collective-permute-start.1) | collective-permute-done | bytes 4128 | tf_op jit(solution)/shard_map/ppermute | solution.py:30
  8.0 0.3 collective-permute-done.other_raw
  8.3 0.0 copy-start.1
  8.3 2.2 %copy-done.1 = bf16[2048,1024]{1,0:T(8,128)(2,1)S(1)} copy-done((bf16[2048,1024]{1,0:T(8,128)(2,1)S(1)}, bf16[2048,1024]{1,0:T(8,128)(2,1)}, u32[]{:S(2)}) %copy-start.1) | copy-done | bytes 4194328
  10.5 13.9 %local.1 = (bf16[2048,1024]{1,0:T(8,128)(2,1)S(1)}, bf16[2048,1024]{1,0:T(8,128)(2,1)S(1)}, f32[512,1024]{1,0:T(8,128)S(1)}, f32[1,512]{1,0:T(1,128)S(1)}, f32[1,2048]{1,0:T(1,128)S(1)}, /*index=5*/f32[1,2048]{1,0:T(1,128)S(1)}) custom-call(s32[1]{0:T(128)} %bitcast.odd, bf16[2048,1024]{1,0:T(8,128)(2,1)S(1)} %copy-done.1, ...), custom_call_target="tpu_custom_call" | custom-call | flops 1000 | bytes 1000 | tf_op jit(solution)/shard_map/local/pallas_call | solution.py:239
  24.4 0.0 collective-permute-done.3.codes.scales
  24.5 2.9 %moved0.1 = (bf16[256,1024]{1,0:T(8,128)(2,1)S(1)}, f32[1,512]{1,0:T(1,128)S(1)}, f32[1,2048]{1,0:T(1,128)S(1)}, f32[1,2048]{1,0:T(1,128)S(1)}) custom-call(s32[1]{0:T(128)} %bitcast.odd, bf16[272,1024]{1,0:T(8,128)(2,1)S(1)} %collective-permute-done.3.codes.scales, bf16[272,1024]{1,0:T(8,128)(2,1)S(1)} %collective-permute-done.3.codes.scales, ...), custom_call_target="tpu_custom_call" | custom-call | flops 1000 | bytes 1000 | tf_op jit(solution)/shard_map/moved0/pallas_call | solution.py:257
  27.3 7.1 %collective-permute-start.5 = (bf16[256,1024]{1,0:T(8,128)(2,1)S(1)}, bf16[256,1024]{1,0:T(8,128)(2,1)S(1)}, u32[]{:S(2)}, u32[]{:S(2)}) collective-permute-start(bf16[256,1024]{1,0:T(8,128)(2,1)S(1)} %get-tuple-element.34), channel_id=1, source_target_pairs={{0,30},{1,31},{2,0},{3,1},{4,2},{5,3},{6,4},{7,5},{8,6},{9,7},{10,... | collective-permute-start | bytes 1572872 | tf_op jit(solution)/shard_map/ppermute | solution.py:25
  34.5 0.0 collective-permute-done.2.codes
  34.5 2.9 %moved1.1 = (bf16[256,1024]{1,0:T(8,128)(2,1)S(1)}, f32[1,512]{1,0:T(1,128)S(1)}, f32[1,2048]{1,0:T(1,128)S(1)}, f32[1,2048]{1,0:T(1,128)S(1)}) custom-call(s32[1]{0:T(128)} %bitcast.odd, bf16[256,1024]{1,0:T(8,128)(2,1)S(1)} %collective-permute-done.2.codes, bf16[272,1024]{1,0:T(8,128)(2,1)S(1)} %collective-permute-done.3.codes.scales, ...), custom_call_target="tpu_custom_call" | custom-call | flops 1000 | bytes 1000 | tf_op jit(solution)/shard_map/moved1/pallas_call | solution.py:257
  37.3 1.3 %collective-permute-start.4 = (bf16[256,1024]{1,0:T(8,128)(2,1)S(1)}, bf16[256,1024]{1,0:T(8,128)(2,1)S(1)}, u32[]{:S(2)}, u32[]{:S(2)}) collective-permute-start(bf16[256,1024]{1,0:T(8,128)(2,1)S(1)} %get-tuple-element.32), channel_id=1, source_target_pairs={{0,30},{1,31},{2,0},{3,1},{4,2},{5,3},{6,4},{7,5},{8,6},{9,7},{10,... | collective-permute-start | bytes 1572872 | tf_op jit(solution)/shard_map/ppermute | solution.py:25
  38.6 7.1 %collective-permute-done.5.back = bf16[256,1024]{1,0:T(8,128)(2,1)S(1)} collective-permute-done((bf16[256,1024]{1,0:T(8,128)(2,1)S(1)}, bf16[256,1024]{1,0:T(8,128)(2,1)S(1)}, u32[]{:S(2)}, u32[]{:S(2)}) %collective-permute-start.5) | collective-permute-done | bytes 524320 | tf_op jit(solution)/shard_map/ppermute | solution.py:25
  45.7 0.0 collective-permute-start.6
  45.7 6.1 %collective-permute-start.7 = (f32[1,512]{1,0:T(1,128)S(1)}, f32[1,512]{1,0:T(1,128)S(1)}, u32[]{:S(2)}, u32[]{:S(2)}) collective-permute-start(f32[1,512]{1,0:T(1,128)S(1)} %get-tuple-element.40), channel_id=1, source_target_pairs={{0,30},{1,31},{2,0},{3,1},{4,2},{5,3},{6,4},{7,5},{8,6},{9,7},{10,... | collective-permute-start | bytes 6152 | tf_op jit(solution)/shard_map/ppermute | solution.py:25
  51.8 1.1 %finish0.1.before = f32[512,1024]{1,0:T(8,128)} custom-call(f32[512,1024]{1,0:T(8,128)S(1)} %get-tuple-element.24.numer, bf16[256,1024]{1,0:T(8,128)(2,1)S(1)} %collective-permute-done.5.back), custom_call_target="tpu_custom_call" | custom-call | flops 1000 | bytes 1000 | tf_op jit(solution)/shard_map/finish0/pallas_call | solution.py:205
  52.9 0.0 collective-permute-done.6
  52.9 0.6 %add_log_fusion = f32[1,2048]{1,0:T(1,128)} fusion(f32[1,2048]{1,0:T(1,128)S(1)} %get-tuple-element.33, f32[1,2048]{1,0:T(1,128)S(1)} %collective-permute-done.6), kind=kLoop, calls=%fused_computation.2 | loop fusion | flops 2048 | bytes 24576 | tf_op jit(solution)/shard_map/log | solution.py:269
  53.5 0.8 %collective-permute-done.4.back = bf16[256,1024]{1,0:T(8,128)(2,1)S(1)} collective-permute-done((bf16[256,1024]{1,0:T(8,128)(2,1)S(1)}, bf16[256,1024]{1,0:T(8,128)(2,1)S(1)}, u32[]{:S(2)}, u32[]{:S(2)}) %collective-permute-start.4) | collective-permute-done | bytes 524320 | tf_op jit(solution)/shard_map/ppermute | solution.py:25
  54.3 0.0 collective-permute-done.7.back_sums
  54.3 1.1 %finish256.1 = (f32[512,1024]{1,0:T(8,128)}, f32[1,512]{1,0:T(1,128)}) custom-call(f32[512,1024]{1,0:T(8,128)S(1)} %get-tuple-element.24.numer, bf16[256,1024]{1,0:T(8,128)(2,1)S(1)} %collective-permute-done.4.back, f32[1,512]{1,0:T(1,128)S(1)} %get-tuple-element.39.sums, ...), custom_call_target="tpu_custom_call", output_to_operand_aliasing={{0}: (4, {})} | custom-call | flops 1000 | bytes 1000 | tf_op jit(solution)/shard_map/finish256/pallas_call | solution.py:205
  (6 shorter events, 0.1 us)
Async XLA Ops:
  0.6 6.0 %copy-start.2 = (bf16[512]{0:T(512)(128)(2,1)S(1)}, bf16[512]{0:T(512)(128)(2,1)}, u32[]{:S(2)}) copy-start(bf16[512]{0:T(512)(128)(2,1)} %param.6) | copy-start | bytes 3076
  0.6 4.4 %copy-start = (bf16[512,1024]{1,0:T(8,128)(2,1)S(1)}, bf16[512,1024]{1,0:T(8,128)(2,1)}, u32[]{:S(2)}) copy-start(bf16[512,1024]{1,0:T(8,128)(2,1)} %own_codes.1) | copy-start | bytes 3145732
  0.7 6.0 %copy-start.3 = (bf16[2048]{0:T(1024)(128)(2,1)S(1)}, bf16[2048]{0:T(1024)(128)(2,1)}, u32[]{:S(2)}) copy-start(bf16[2048]{0:T(1024)(128)(2,1)} %param.7) | copy-start | bytes 12292
  0.7 7.6 %collective-permute-start = (bf16[2048,1024]{1,0:T(8,128)(2,1)}, bf16[2048,1024]{1,0:T(8,128)(2,1)}, u32[]{:S(2)}, u32[]{:S(2)}) collective-permute-start(bf16[2048,1024]{1,0:T(8,128)(2,1)} %own_raw.1), channel_id=1, source_target_pairs={{0,1},{1,0},{2,3},{3,2},{4,5},{5,4},{6,7},{7,6},{8,9},{9,8},{10,11... | collective-permute-start | bytes 12582920 | tf_op jit(solution)/shard_map/ppermute | solution.py:30
  2.4 22.0 %collective-permute-start.3 = (bf16[272,1024]{1,0:T(8,128)(2,1)S(1)}, bf16[272,1024]{1,0:T(8,128)(2,1)S(1)}, u32[]{:S(2)}, u32[]{:S(2)}) collective-permute-start(bf16[272,1024]{1,0:T(8,128)(2,1)S(1)} %pad_maximum_fusion), channel_id=1, source_target_pairs={{0,2},{1,3},{2,4},{3,5},{4,6},{5,7},{6,8},{7,9},{8,10},{9,11},{10,... | collective-permute-start | bytes 1671176 | tf_op jit(solution)/shard_map/ppermute | solution.py:25
  5.1 29.4 %collective-permute-start.2 = (bf16[256,1024]{1,0:T(8,128)(2,1)S(1)}, bf16[256,1024]{1,0:T(8,128)(2,1)S(1)}, u32[]{:S(2)}, u32[]{:S(2)}) collective-permute-start(bf16[256,1024]{1,0:T(8,128)(2,1)S(1)} %slice.15), channel_id=1, source_target_pairs={{0,2},{1,3},{2,4},{3,5},{4,6},{5,7},{6,8},{7,9},{8,10},{9,11},{10,... | collective-permute-start | bytes 1572872 | tf_op jit(solution)/shard_map/ppermute | solution.py:25
  6.6 1.3 %collective-permute-start.1 = (bf16[2048]{0:T(1024)(128)(2,1)S(1)}, bf16[2048]{0:T(1024)(128)(2,1)S(1)}, u32[]{:S(2)}, u32[]{:S(2)}) collective-permute-start(bf16[2048]{0:T(1024)(128)(2,1)S(1)} %copy-done.3), channel_id=1, source_target_pairs={{0,1},{1,0},{2,3},{3,2},{4,5},{5,4},{6,7},{7,6},{8,9},{9,8},{10,11... | collective-permute-start | bytes 12296 | tf_op jit(solution)/shard_map/ppermute | solution.py:30
  8.3 2.2 %copy-start.1 = (bf16[2048,1024]{1,0:T(8,128)(2,1)S(1)}, bf16[2048,1024]{1,0:T(8,128)(2,1)}, u32[]{:S(2)}) copy-start(bf16[2048,1024]{1,0:T(8,128)(2,1)} %own_raw.1) | copy-start | bytes 12582916
  27.3 18.3 %collective-permute-start.5 = (bf16[256,1024]{1,0:T(8,128)(2,1)S(1)}, bf16[256,1024]{1,0:T(8,128)(2,1)S(1)}, u32[]{:S(2)}, u32[]{:S(2)}) collective-permute-start(bf16[256,1024]{1,0:T(8,128)(2,1)S(1)} %get-tuple-element.34), channel_id=1, source_target_pairs={{0,30},{1,31},{2,0},{3,1},{4,2},{5,3},{6,4},{7,5},{8,6},{9,7},{10,... | collective-permute-start | bytes 1572872 | tf_op jit(solution)/shard_map/ppermute | solution.py:25
  37.3 17.0 %collective-permute-start.4 = (bf16[256,1024]{1,0:T(8,128)(2,1)S(1)}, bf16[256,1024]{1,0:T(8,128)(2,1)S(1)}, u32[]{:S(2)}, u32[]{:S(2)}) collective-permute-start(bf16[256,1024]{1,0:T(8,128)(2,1)S(1)} %get-tuple-element.32), channel_id=1, source_target_pairs={{0,30},{1,31},{2,0},{3,1},{4,2},{5,3},{6,4},{7,5},{8,6},{9,7},{10,... | collective-permute-start | bytes 1572872 | tf_op jit(solution)/shard_map/ppermute | solution.py:25
  45.7 7.2 %collective-permute-start.6 = (f32[1,2048]{1,0:T(1,128)S(1)}, f32[1,2048]{1,0:T(1,128)S(1)}, u32[]{:S(2)}, u32[]{:S(2)}) collective-permute-start(f32[1,2048]{1,0:T(1,128)S(1)} %get-tuple-element.37), channel_id=1, source_target_pairs={{0,1},{1,0},{2,3},{3,2},{4,5},{5,4},{6,7},{7,6},{8,9},{9,8},{10,11... | collective-permute-start | bytes 24584 | tf_op jit(solution)/shard_map/ppermute | solution.py:30
  45.7 8.7 %collective-permute-start.7 = (f32[1,512]{1,0:T(1,128)S(1)}, f32[1,512]{1,0:T(1,128)S(1)}, u32[]{:S(2)}, u32[]{:S(2)}) collective-permute-start(f32[1,512]{1,0:T(1,128)S(1)} %get-tuple-element.40), channel_id=1, source_target_pairs={{0,30},{1,31},{2,0},{3,1},{4,2},{5,3},{6,4},{7,5},{8,6},{9,7},{10,... | collective-permute-start | bytes 6152 | tf_op jit(solution)/shard_map/ppermute | solution.py:25

commit v4 on v3

--- a/solution.py
+++ b/solution.py
@@ -228,6 +228,7 @@
     first = jnp.concatenate(
         [jnp.where(row < cuts[0].stop, first[:, :rows], centroid_scales), first[:, rows:]], axis=1
     )
+    first, embeddings = lax.optimization_barrier((first, embeddings))
     received = [shift(first, 2)]
     received += [shift(lax.optimization_barrier(centroid_codes)[cut], 2) for cut in cuts[1:]]
     scales = centroid_scales.astype(F32).reshape(1, rows)
@@ -248,7 +249,7 @@
         ],
         [SMEM, HBM, HBM, HBM] + [VMEM] * 3,
         "local",
-        mib=24,
+        mib=40,
     )(odd, embeddings, other_raw, centroid_codes, scales, logs, other_logs)
     back = []
     sums = jnp.zeros((1, rows), F32)

time: 55.7 us -> 55.5 us (level)
  local copies, waits for them, and re-layouts: 2.24 us -> 0.06 us
  waiting for transfers between devices: 9.54 us -> 10.7 us
  Pallas kernels: 21.9 us -> 22.7 us
    unnamed x8 -> x6, local copies, waits for them, and re-layouts: 2.2 us -> 0.02 us
    ppermute x3, waiting for transfers between devices: 1.65 us -> 2.95 us  [partner(): return lax.ppermute(value, 'blk', [(i, i ^ 1) for i in range(count)])]
    pallas_call x1, Pallas kernels: 13.9 us -> 14.7 us  [on_device(): call(functools.partial(local_kernel, half), [units, units, ((rows, width)...]
  transfers between devices with their start and end apart: 8 -> 8, of which waited for: 4 -> 4; matrix products, arithmetic and copies ran while one was open for 3% -> 1% of each run, Pallas kernels for 37% -> 39%
where the time goes in v4:
time: 55.5 us; the launch traced here: 55.3 us
  Pallas kernels  22.7 us (41%)
  starting transfers between devices  19.3 us (35%)
  waiting for transfers between devices  10.7 us (19%)
  other arithmetic  1.92 us (3%)
  between operations  0.76 us (1%)
    ppermute x5, starting transfers between devices, shift(): lax.ppermute(value, 'blk', [(i, (i + steps) % count) for i in range(count)])  18.7 us
    pallas_call x1, Pallas kernels, on_device(): call(functools.partial(local_kernel, half), [units, units, ((rows, width)...  14.7 us
    ppermute x5, waiting for transfers between devices, shift(): lax.ppermute(value, 'blk', [(i, (i + steps) % count) for i in range(count)])  7.73 us
    pallas_call x2, Pallas kernels, on_device(): call(functools.partial(moved_kernel, cut), [((part, width), BF16), ((1, r...  5.73 us
    ppermute x3, waiting for transfers between devices, partner(): return lax.ppermute(value, 'blk', [(i, i ^ 1) for i in range(count)])  2.95 us
    pallas_call x2, Pallas kernels, finish(): pl.pallas_call(functools.partial(last_rows if more else first_rows, cut),...  2.27 us
    select_n x1, other arithmetic, on_device(): jnp.where(row < cuts[0].stop, first[:, :rows], centroid_scales)  1.23 us
  transfers between devices with their start and end apart: 8, of which 4 were waited for; matrix products, arithmetic and copies ran while one was open for 1% of the time, Pallas kernels for 39%

profile of v4, /device:TPU:0, one launch (start us, length us, event | category | flops | bytes accessed | tf_op | source)
XLA Modules:
  0.0 55.3 jit_solution(11328379825125344187)
XLA Ops:
  0.6 0.0 copy-start
  0.6 0.0 copy-start.1
  0.7 0.0 copy-start.2
  0.7 1.2 %slice_select_fusion = (bf16[272,512]{1,0:T(8,128)(2,1)S(1)}, bf16[272,512]{1,0:T(8,128)(2,1)S(1)}) fusion(bf16[512,1024]{1,0:T(8,128)(2,1)} %own_codes.1, pred[272]{0:T(512)(128)(4,1)S(1)} %iota_compare_fusion, bf16[512]{0:T(512)(128)(2,1)} %param.6), kind=kLoop, calls=%fused_computation.1 | loop fusion | flops 139264 | bytes 1115408 | tf_op jit(solution)/shard_map/jit(_where)/select_n | solution.py:229
  1.9 0.1 pad_maximum_fusion
  2.0 0.5 collective-permute-start
  2.5 2.6 %collective-permute-start.3 = (bf16[272,1024]{1,0:T(8,128)(2,1)S(1)}, bf16[272,1024]{1,0:T(8,128)(2,1)S(1)}, u32[]{:S(2)}, u32[]{:S(2)}) collective-permute-start(bf16[272,1024]{1,0:T(8,128)(2,1)S(1)} %pad_maximum_fusion), channel_id=1, source_target_pairs={{0,2},{1,3},{2,4},{3,5},{4,6},{5,7},{6,8},{7,9},{8,10},{9,11},{10,... | collective-permute-start | bytes 1671176 | tf_op jit(solution)/shard_map/ppermute | solution.py:25
  5.1 0.0 copy-done
  5.1 1.5 %collective-permute-start.2 = (bf16[256,1024]{1,0:T(8,128)(2,1)S(1)}, bf16[256,1024]{1,0:T(8,128)(2,1)S(1)}, u32[]{:S(2)}, u32[]{:S(2)}) collective-permute-start(bf16[256,1024]{1,0:T(8,128)(2,1)S(1)} %slice.15), channel_id=1, source_target_pairs={{0,2},{1,3},{2,4},{3,5},{4,6},{5,7},{6,8},{7,9},{8,10},{9,11},{10,... | collective-permute-start | bytes 1572872 | tf_op jit(solution)/shard_map/ppermute | solution.py:25
  6.6 0.0 copy-done.2
  6.6 0.0 collective-permute-start.1
  6.7 0.0 copy-done.1
  6.7 2.6 %collective-permute-done.1 = bf16[2048]{0:T(1024)(128)(2,1)S(1)} collective-permute-done((bf16[2048]{0:T(1024)(128)(2,1)S(1)}, bf16[2048]{0:T(1024)(128)(2,1)S(1)}, u32[]{:S(2)}, u32[]{:S(2)}) %collective-permute-start.1) | collective-permute-done | bytes 4128 | tf_op jit(solution)/shard_map/ppermute | solution.py:30
  9.3 0.3 collective-permute-done.other_raw
  9.6 14.7 %local.1 = (bf16[2048,1024]{1,0:T(8,128)(2,1)S(1)}, bf16[2048,1024]{1,0:T(8,128)(2,1)S(1)}, f32[512,1024]{1,0:T(8,128)S(1)}, f32[1,512]{1,0:T(1,128)S(1)}, f32[1,2048]{1,0:T(1,128)S(1)}, /*index=5*/f32[1,2048]{1,0:T(1,128)S(1)}) custom-call(s32[1]{0:T(128)} %bitcast.odd, bf16[2048,1024]{1,0:T(8,128)(2,1)} %own_raw, ...), custom_call_target="tpu_custom_call" | custom-call | flops 1000 | bytes 1000 | tf_op jit(solution)/shard_map/local/pallas_call | solution.py:240
  24.3 0.0 collective-permute-done.3.codes.scales
  24.3 2.9 %moved0.1 = (bf16[256,1024]{1,0:T(8,128)(2,1)S(1)}, f32[1,512]{1,0:T(1,128)S(1)}, f32[1,2048]{1,0:T(1,128)S(1)}, f32[1,2048]{1,0:T(1,128)S(1)}) custom-call(s32[1]{0:T(128)} %bitcast.odd, bf16[272,1024]{1,0:T(8,128)(2,1)S(1)} %collective-permute-done.3.codes.scales, bf16[272,1024]{1,0:T(8,128)(2,1)S(1)} %collective-permute-done.3.codes.scales, ...), custom_call_target="tpu_custom_call" | custom-call | flops 1000 | bytes 1000 | tf_op jit(solution)/shard_map/moved0/pallas_call | solution.py:258
  27.2 7.1 %collective-permute-start.5 = (bf16[256,1024]{1,0:T(8,128)(2,1)S(1)}, bf16[256,1024]{1,0:T(8,128)(2,1)S(1)}, u32[]{:S(2)}, u32[]{:S(2)}) collective-permute-start(bf16[256,1024]{1,0:T(8,128)(2,1)S(1)} %get-tuple-element.38), channel_id=1, source_target_pairs={{0,30},{1,31},{2,0},{3,1},{4,2},{5,3},{6,4},{7,5},{8,6},{9,7},{10,... | collective-permute-start | bytes 1572872 | tf_op jit(solution)/shard_map/ppermute | solution.py:25
  34.3 0.0 collective-permute-done.2.codes
  34.3 2.9 %moved1.1 = (bf16[256,1024]{1,0:T(8,128)(2,1)S(1)}, f32[1,512]{1,0:T(1,128)S(1)}, f32[1,2048]{1,0:T(1,128)S(1)}, f32[1,2048]{1,0:T(1,128)S(1)}) custom-call(s32[1]{0:T(128)} %bitcast.odd, bf16[256,1024]{1,0:T(8,128)(2,1)S(1)} %collective-permute-done.2.codes, bf16[272,1024]{1,0:T(8,128)(2,1)S(1)} %collective-permute-done.3.codes.scales, ...), custom_call_target="tpu_custom_call" | custom-call | flops 1000 | bytes 1000 | tf_op jit(solution)/shard_map/moved1/pallas_call | solution.py:258
  37.2 1.4 %collective-permute-start.4 = (bf16[256,1024]{1,0:T(8,128)(2,1)S(1)}, bf16[256,1024]{1,0:T(8,128)(2,1)S(1)}, u32[]{:S(2)}, u32[]{:S(2)}) collective-permute-start(bf16[256,1024]{1,0:T(8,128)(2,1)S(1)} %get-tuple-element.36), channel_id=1, source_target_pairs={{0,30},{1,31},{2,0},{3,1},{4,2},{5,3},{6,4},{7,5},{8,6},{9,7},{10,... | collective-permute-start | bytes 1572872 | tf_op jit(solution)/shard_map/ppermute | solution.py:25
  38.6 6.7 %collective-permute-done.5.back = bf16[256,1024]{1,0:T(8,128)(2,1)S(1)} collective-permute-done((bf16[256,1024]{1,0:T(8,128)(2,1)S(1)}, bf16[256,1024]{1,0:T(8,128)(2,1)S(1)}, u32[]{:S(2)}, u32[]{:S(2)}) %collective-permute-start.5) | collective-permute-done | bytes 524320 | tf_op jit(solution)/shard_map/ppermute | solution.py:25
  45.4 0.0 collective-permute-start.6
  45.4 6.1 %collective-permute-start.7 = (f32[1,512]{1,0:T(1,128)S(1)}, f32[1,512]{1,0:T(1,128)S(1)}, u32[]{:S(2)}, u32[]{:S(2)}) collective-permute-start(f32[1,512]{1,0:T(1,128)S(1)} %get-tuple-element.44), channel_id=1, source_target_pairs={{0,30},{1,31},{2,0},{3,1},{4,2},{5,3},{6,4},{7,5},{8,6},{9,7},{10,... | collective-permute-start | bytes 6152 | tf_op jit(solution)/shard_map/ppermute | solution.py:25
  51.4 1.1 %finish0.1.before = f32[512,1024]{1,0:T(8,128)} custom-call(f32[512,1024]{1,0:T(8,128)S(1)} %get-tuple-element.27.numer, bf16[256,1024]{1,0:T(8,128)(2,1)S(1)} %collective-permute-done.5.back), custom_call_target="tpu_custom_call" | custom-call | flops 1000 | bytes 1000 | tf_op jit(solution)/shard_map/finish0/pallas_call | solution.py:205
  52.6 0.0 collective-permute-done.6
  52.6 0.6 %add_log_fusion = f32[1,2048]{1,0:T(1,128)} fusion(f32[1,2048]{1,0:T(1,128)S(1)} %get-tuple-element.37, f32[1,2048]{1,0:T(1,128)S(1)} %collective-permute-done.6), kind=kLoop, calls=%fused_computation.2 | loop fusion | flops 2048 | bytes 24576 | tf_op jit(solution)/shard_map/log | solution.py:270
  53.2 1.0 %collective-permute-done.4.back = bf16[256,1024]{1,0:T(8,128)(2,1)S(1)} collective-permute-done((bf16[256,1024]{1,0:T(8,128)(2,1)S(1)}, bf16[256,1024]{1,0:T(8,128)(2,1)S(1)}, u32[]{:S(2)}, u32[]{:S(2)}) %collective-permute-start.4) | collective-permute-done | bytes 524320 | tf_op jit(solution)/shard_map/ppermute | solution.py:25
  54.2 0.0 collective-permute-done.7.back_sums
  54.2 1.1 %finish256.1 = (f32[512,1024]{1,0:T(8,128)}, f32[1,512]{1,0:T(1,128)}) custom-call(f32[512,1024]{1,0:T(8,128)S(1)} %get-tuple-element.27.numer, bf16[256,1024]{1,0:T(8,128)(2,1)S(1)} %collective-permute-done.4.back, f32[1,512]{1,0:T(1,128)S(1)} %get-tuple-element.43.sums, ...), custom_call_target="tpu_custom_call", output_to_operand_aliasing={{0}: (4, {})} | custom-call | flops 1000 | bytes 1000 | tf_op jit(solution)/shard_map/finish256/pallas_call | solution.py:205
  (6 shorter events, 0.1 us)
Async XLA Ops:
  0.6 4.4 %copy-start = (bf16[512,1024]{1,0:T(8,128)(2,1)S(1)}, bf16[512,1024]{1,0:T(8,128)(2,1)}, u32[]{:S(2)}) copy-start(bf16[512,1024]{1,0:T(8,128)(2,1)} %own_codes.1) | copy-start | bytes 3145732
  0.6 6.0 %copy-start.1 = (bf16[512]{0:T(512)(128)(2,1)S(1)}, bf16[512]{0:T(512)(128)(2,1)}, u32[]{:S(2)}) copy-start(bf16[512]{0:T(512)(128)(2,1)} %param.6) | copy-start | bytes 3076
  0.7 6.0 %copy-start.2 = (bf16[2048]{0:T(1024)(128)(2,1)S(1)}, bf16[2048]{0:T(1024)(128)(2,1)}, u32[]{:S(2)}) copy-start(bf16[2048]{0:T(1024)(128)(2,1)} %param.7) | copy-start | bytes 12292
  2.0 7.6 %collective-permute-start = (bf16[2048,1024]{1,0:T(8,128)(2,1)}, bf16[2048,1024]{1,0:T(8,128)(2,1)}, u32[]{:S(2)}, u32[]{:S(2)}) collective-permute-start(bf16[2048,1024]{1,0:T(8,128)(2,1)} %own_raw), channel_id=1, source_target_pairs={{0,1},{1,0},{2,3},{3,2},{4,5},{5,4},{6,7},{7,6},{8,9},{9,8},{10,11... | collective-permute-start | bytes 12582920 | tf_op jit(solution)/shard_map/ppermute | solution.py:30
  2.5 21.8 %collective-permute-start.3 = (bf16[272,1024]{1,0:T(8,128)(2,1)S(1)}, bf16[272,1024]{1,0:T(8,128)(2,1)S(1)}, u32[]{:S(2)}, u32[]{:S(2)}) collective-permute-start(bf16[272,1024]{1,0:T(8,128)(2,1)S(1)} %pad_maximum_fusion), channel_id=1, source_target_pairs={{0,2},{1,3},{2,4},{3,5},{4,6},{5,7},{6,8},{7,9},{8,10},{9,11},{10,... | collective-permute-start | bytes 1671176 | tf_op jit(solution)/shard_map/ppermute | solution.py:25
  5.1 29.2 %collective-permute-start.2 = (bf16[256,1024]{1,0:T(8,128)(2,1)S(1)}, bf16[256,1024]{1,0:T(8,128)(2,1)S(1)}, u32[]{:S(2)}, u32[]{:S(2)}) collective-permute-start(bf16[256,1024]{1,0:T(8,128)(2,1)S(1)} %slice.15), channel_id=1, source_target_pairs={{0,2},{1,3},{2,4},{3,5},{4,6},{5,7},{6,8},{7,9},{8,10},{9,11},{10,... | collective-permute-start | bytes 1572872 | tf_op jit(solution)/shard_map/ppermute | solution.py:25
  6.6 2.6 %collective-permute-start.1 = (bf16[2048]{0:T(1024)(128)(2,1)S(1)}, bf16[2048]{0:T(1024)(128)(2,1)S(1)}, u32[]{:S(2)}, u32[]{:S(2)}) collective-permute-start(bf16[2048]{0:T(1024)(128)(2,1)S(1)} %copy-done.2), channel_id=1, source_target_pairs={{0,1},{1,0},{2,3},{3,2},{4,5},{5,4},{6,7},{7,6},{8,9},{9,8},{10,11... | collective-permute-start | bytes 12296 | tf_op jit(solution)/shard_map/ppermute | solution.py:30
  27.2 18.1 %collective-permute-start.5 = (bf16[256,1024]{1,0:T(8,128)(2,1)S(1)}, bf16[256,1024]{1,0:T(8,128)(2,1)S(1)}, u32[]{:S(2)}, u32[]{:S(2)}) collective-permute-start(bf16[256,1024]{1,0:T(8,128)(2,1)S(1)} %get-tuple-element.38), channel_id=1, source_target_pairs={{0,30},{1,31},{2,0},{3,1},{4,2},{5,3},{6,4},{7,5},{8,6},{9,7},{10,... | collective-permute-start | bytes 1572872 | tf_op jit(solution)/shard_map/ppermute | solution.py:25
  37.2 17.0 %collective-permute-start.4 = (bf16[256,1024]{1,0:T(8,128)(2,1)S(1)}, bf16[256,1024]{1,0:T(8,128)(2,1)S(1)}, u32[]{:S(2)}, u32[]{:S(2)}) collective-permute-start(bf16[256,1024]{1,0:T(8,128)(2,1)S(1)} %get-tuple-element.36), channel_id=1, source_target_pairs={{0,30},{1,31},{2,0},{3,1},{4,2},{5,3},{6,4},{7,5},{8,6},{9,7},{10,... | collective-permute-start | bytes 1572872 | tf_op jit(solution)/shard_map/ppermute | solution.py:25
  45.4 7.2 %collective-permute-start.6 = (f32[1,2048]{1,0:T(1,128)S(1)}, f32[1,2048]{1,0:T(1,128)S(1)}, u32[]{:S(2)}, u32[]{:S(2)}) collective-permute-start(f32[1,2048]{1,0:T(1,128)S(1)} %get-tuple-element.41), channel_id=1, source_target_pairs={{0,1},{1,0},{2,3},{3,2},{4,5},{5,4},{6,7},{7,6},{8,9},{9,8},{10,11... | collective-permute-start | bytes 24584 | tf_op jit(solution)/shard_map/ppermute | solution.py:30
  45.4 8.8 %collective-permute-start.7 = (f32[1,512]{1,0:T(1,128)S(1)}, f32[1,512]{1,0:T(1,128)S(1)}, u32[]{:S(2)}, u32[]{:S(2)}) collective-permute-start(f32[1,512]{1,0:T(1,128)S(1)} %get-tuple-element.44), channel_id=1, source_target_pairs={{0,30},{1,31},{2,0},{3,1},{4,2},{5,3},{6,4},{7,5},{8,6},{9,7},{10,... | collective-permute-start | bytes 6152 | tf_op jit(solution)/shard_map/ppermute | solution.py:25

commit v5 on v3

--- a/solution.py
+++ b/solution.py
@@ -10,7 +10,7 @@
 HALVES = 2
 SIZES = (256, 256)
 EXTRA = 16
-TILE = 512
+TILE = 1024
 LANES = 128
 NORM = 256
 F32 = jnp.float32

time: 55.7 us -> 55.2 us (level)
    pallas_call x1, Pallas kernels: 13.9 us -> 13.4 us  [on_device(): call(functools.partial(local_kernel, half), [units, units, ((rows, width)...]
where the time goes in v5:
time: 55.2 us; the launch traced here: 55 us
  Pallas kernels  21.4 us (39%)
  starting transfers between devices  19.7 us (36%)
  waiting for transfers between devices  9.05 us (16%)
  local copies, waits for them, and re-layouts  2.24 us (4%)
  other arithmetic  1.83 us (3%)
  between operations  0.75 us (1%)
    ppermute x5, starting transfers between devices, shift(): lax.ppermute(value, 'blk', [(i, (i + steps) % count) for i in range(count)])  19.2 us
    pallas_call x1, Pallas kernels, on_device(): call(functools.partial(local_kernel, half), [units, units, ((rows, width)...  13.4 us
    ppermute x5, waiting for transfers between devices, shift(): lax.ppermute(value, 'blk', [(i, (i + steps) % count) for i in range(count)])  7.41 us
    pallas_call x2, Pallas kernels, on_device(): call(functools.partial(moved_kernel, cut), [((part, width), BF16), ((1, r...  5.76 us
    pallas_call x2, Pallas kernels, finish(): pl.pallas_call(functools.partial(last_rows if more else first_rows, cut),...  2.27 us
    unnamed x8, local copies, waits for them, and re-layouts  2.2 us
    ppermute x3, waiting for transfers between devices, partner(): return lax.ppermute(value, 'blk', [(i, i ^ 1) for i in range(count)])  1.65 us
    select_n x1, other arithmetic, on_device(): jnp.where(row < cuts[0].stop, first[:, :rows], centroid_scales)  1.14 us
  transfers between devices with their start and end apart: 8, of which 4 were waited for; matrix products, arithmetic and copies ran while one was open for 3% of the time, Pallas kernels for 37%

profile of v5, /device:TPU:0, one launch (start us, length us, event | category | flops | bytes accessed | tf_op | source)
XLA Modules:
  0.0 55.0 jit_solution(1590366869227965416)
XLA Ops:
  0.6 0.0 copy-start.2
  0.6 0.0 copy-start
  0.7 0.0 copy-start.3
  0.7 0.5 collective-permute-start
  1.2 1.1 %slice_select_fusion = (bf16[272,512]{1,0:T(8,128)(2,1)S(1)}, bf16[272,512]{1,0:T(8,128)(2,1)S(1)}) fusion(bf16[512,1024]{1,0:T(8,128)(2,1)} %own_codes.1, pred[272]{0:T(512)(128)(4,1)S(1)} %iota_compare_fusion, bf16[512]{0:T(512)(128)(2,1)} %param.6), kind=kLoop, calls=%fused_computation.1 | loop fusion | flops 139264 | bytes 1115408 | tf_op jit(solution)/shard_map/jit(_where)/select_n | solution.py:229
  2.3 0.1 pad_maximum_fusion
  2.4 2.6 %collective-permute-start.3 = (bf16[272,1024]{1,0:T(8,128)(2,1)S(1)}, bf16[272,1024]{1,0:T(8,128)(2,1)S(1)}, u32[]{:S(2)}, u32[]{:S(2)}) collective-permute-start(bf16[272,1024]{1,0:T(8,128)(2,1)S(1)} %pad_maximum_fusion), channel_id=1, source_target_pairs={{0,2},{1,3},{2,4},{3,5},{4,6},{5,7},{6,8},{7,9},{8,10},{9,11},{10,... | collective-permute-start | bytes 1671176 | tf_op jit(solution)/shard_map/ppermute | solution.py:25
  5.0 0.0 copy-done
  5.1 1.5 %collective-permute-start.2 = (bf16[256,1024]{1,0:T(8,128)(2,1)S(1)}, bf16[256,1024]{1,0:T(8,128)(2,1)S(1)}, u32[]{:S(2)}, u32[]{:S(2)}) collective-permute-start(bf16[256,1024]{1,0:T(8,128)(2,1)S(1)} %slice.15), channel_id=1, source_target_pairs={{0,2},{1,3},{2,4},{3,5},{4,6},{5,7},{6,8},{7,9},{8,10},{9,11},{10,... | collective-permute-start | bytes 1572872 | tf_op jit(solution)/shard_map/ppermute | solution.py:25
  6.6 0.0 copy-done.3
  6.6 0.0 collective-permute-start.1
  6.6 0.0 copy-done.2
  6.7 1.3 %collective-permute-done.1 = bf16[2048]{0:T(1024)(128)(2,1)S(1)} collective-permute-done((bf16[2048]{0:T(1024)(128)(2,1)S(1)}, bf16[2048]{0:T(1024)(128)(2,1)S(1)}, u32[]{:S(2)}, u32[]{:S(2)}) %collective-permute-start.1) | collective-permute-done | bytes 4128 | tf_op jit(solution)/shard_map/ppermute | solution.py:30
  8.0 0.3 collective-permute-done.other_raw
  8.3 0.0 copy-start.1
  8.3 2.2 %copy-done.1 = bf16[2048,1024]{1,0:T(8,128)(2,1)S(1)} copy-done((bf16[2048,1024]{1,0:T(8,128)(2,1)S(1)}, bf16[2048,1024]{1,0:T(8,128)(2,1)}, u32[]{:S(2)}) %copy-start.1) | copy-done | bytes 4194328
  10.5 13.4 %local.1 = (bf16[2048,1024]{1,0:T(8,128)(2,1)S(1)}, bf16[2048,1024]{1,0:T(8,128)(2,1)S(1)}, f32[512,1024]{1,0:T(8,128)S(1)}, f32[1,512]{1,0:T(1,128)S(1)}, f32[1,2048]{1,0:T(1,128)S(1)}, /*index=5*/f32[1,2048]{1,0:T(1,128)S(1)}) custom-call(s32[1]{0:T(128)} %bitcast.odd, bf16[2048,1024]{1,0:T(8,128)(2,1)S(1)} %copy-done.1, ...), custom_call_target="tpu_custom_call" | custom-call | flops 1000 | bytes 1000 | tf_op jit(solution)/shard_map/local/pallas_call | solution.py:239
  23.9 0.0 collective-permute-done.3.codes.scales
  23.9 2.9 %moved0.1 = (bf16[256,1024]{1,0:T(8,128)(2,1)S(1)}, f32[1,512]{1,0:T(1,128)S(1)}, f32[1,2048]{1,0:T(1,128)S(1)}, f32[1,2048]{1,0:T(1,128)S(1)}) custom-call(s32[1]{0:T(128)} %bitcast.odd, bf16[272,1024]{1,0:T(8,128)(2,1)S(1)} %collective-permute-done.3.codes.scales, bf16[272,1024]{1,0:T(8,128)(2,1)S(1)} %collective-permute-done.3.codes.scales, ...), custom_call_target="tpu_custom_call" | custom-call | flops 1000 | bytes 1000 | tf_op jit(solution)/shard_map/moved0/pallas_call | solution.py:257
  26.8 6.9 %collective-permute-start.5 = (bf16[256,1024]{1,0:T(8,128)(2,1)S(1)}, bf16[256,1024]{1,0:T(8,128)(2,1)S(1)}, u32[]{:S(2)}, u32[]{:S(2)}) collective-permute-start(bf16[256,1024]{1,0:T(8,128)(2,1)S(1)} %get-tuple-element.34), channel_id=1, source_target_pairs={{0,30},{1,31},{2,0},{3,1},{4,2},{5,3},{6,4},{7,5},{8,6},{9,7},{10,... | collective-permute-start | bytes 1572872 | tf_op jit(solution)/shard_map/ppermute | solution.py:25
  33.7 0.0 collective-permute-done.2.codes
  33.7 2.9 %moved1.1 = (bf16[256,1024]{1,0:T(8,128)(2,1)S(1)}, f32[1,512]{1,0:T(1,128)S(1)}, f32[1,2048]{1,0:T(1,128)S(1)}, f32[1,2048]{1,0:T(1,128)S(1)}) custom-call(s32[1]{0:T(128)} %bitcast.odd, bf16[256,1024]{1,0:T(8,128)(2,1)S(1)} %collective-permute-done.2.codes, bf16[272,1024]{1,0:T(8,128)(2,1)S(1)} %collective-permute-done.3.codes.scales, ...), custom_call_target="tpu_custom_call" | custom-call | flops 1000 | bytes 1000 | tf_op jit(solution)/shard_map/moved1/pallas_call | solution.py:257
  36.6 2.1 %collective-permute-start.4 = (bf16[256,1024]{1,0:T(8,128)(2,1)S(1)}, bf16[256,1024]{1,0:T(8,128)(2,1)S(1)}, u32[]{:S(2)}, u32[]{:S(2)}) collective-permute-start(bf16[256,1024]{1,0:T(8,128)(2,1)S(1)} %get-tuple-element.32), channel_id=1, source_target_pairs={{0,30},{1,31},{2,0},{3,1},{4,2},{5,3},{6,4},{7,5},{8,6},{9,7},{10,... | collective-permute-start | bytes 1572872 | tf_op jit(solution)/shard_map/ppermute | solution.py:25
  38.6 6.1 %collective-permute-done.5.back = bf16[256,1024]{1,0:T(8,128)(2,1)S(1)} collective-permute-done((bf16[256,1024]{1,0:T(8,128)(2,1)S(1)}, bf16[256,1024]{1,0:T(8,128)(2,1)S(1)}, u32[]{:S(2)}, u32[]{:S(2)}) %collective-permute-start.5) | collective-permute-done | bytes 524320 | tf_op jit(solution)/shard_map/ppermute | solution.py:25
  44.7 0.0 collective-permute-start.6
  44.7 6.1 %collective-permute-start.7 = (f32[1,512]{1,0:T(1,128)S(1)}, f32[1,512]{1,0:T(1,128)S(1)}, u32[]{:S(2)}, u32[]{:S(2)}) collective-permute-start(f32[1,512]{1,0:T(1,128)S(1)} %get-tuple-element.40), channel_id=1, source_target_pairs={{0,30},{1,31},{2,0},{3,1},{4,2},{5,3},{6,4},{7,5},{8,6},{9,7},{10,... | collective-permute-start | bytes 6152 | tf_op jit(solution)/shard_map/ppermute | solution.py:25
  50.8 1.1 %finish0.1.before = f32[512,1024]{1,0:T(8,128)} custom-call(f32[512,1024]{1,0:T(8,128)S(1)} %get-tuple-element.24.numer, bf16[256,1024]{1,0:T(8,128)(2,1)S(1)} %collective-permute-done.5.back), custom_call_target="tpu_custom_call" | custom-call | flops 1000 | bytes 1000 | tf_op jit(solution)/shard_map/finish0/pallas_call | solution.py:205
  52.0 0.0 collective-permute-done.6
  52.0 0.6 %add_log_fusion = f32[1,2048]{1,0:T(1,128)} fusion(f32[1,2048]{1,0:T(1,128)S(1)} %get-tuple-element.33, f32[1,2048]{1,0:T(1,128)S(1)} %collective-permute-done.6), kind=kLoop, calls=%fused_computation.2 | loop fusion | flops 2048 | bytes 24576 | tf_op jit(solution)/shard_map/log | solution.py:269
  52.6 1.3 %collective-permute-done.4.back = bf16[256,1024]{1,0:T(8,128)(2,1)S(1)} collective-permute-done((bf16[256,1024]{1,0:T(8,128)(2,1)S(1)}, bf16[256,1024]{1,0:T(8,128)(2,1)S(1)}, u32[]{:S(2)}, u32[]{:S(2)}) %collective-permute-start.4) | collective-permute-done | bytes 524320 | tf_op jit(solution)/shard_map/ppermute | solution.py:25
  53.9 0.0 collective-permute-done.7.back_sums
  53.9 1.1 %finish256.1 = (f32[512,1024]{1,0:T(8,128)}, f32[1,512]{1,0:T(1,128)}) custom-call(f32[512,1024]{1,0:T(8,128)S(1)} %get-tuple-element.24.numer, bf16[256,1024]{1,0:T(8,128)(2,1)S(1)} %collective-permute-done.4.back, f32[1,512]{1,0:T(1,128)S(1)} %get-tuple-element.39.sums, ...), custom_call_target="tpu_custom_call", output_to_operand_aliasing={{0}: (4, {})} | custom-call | flops 1000 | bytes 1000 | tf_op jit(solution)/shard_map/finish256/pallas_call | solution.py:205
  (6 shorter events, 0.1 us)
Async XLA Ops:
  0.6 6.0 %copy-start.2 = (bf16[512]{0:T(512)(128)(2,1)S(1)}, bf16[512]{0:T(512)(128)(2,1)}, u32[]{:S(2)}) copy-start(bf16[512]{0:T(512)(128)(2,1)} %param.6) | copy-start | bytes 3076
  0.6 4.4 %copy-start = (bf16[512,1024]{1,0:T(8,128)(2,1)S(1)}, bf16[512,1024]{1,0:T(8,128)(2,1)}, u32[]{:S(2)}) copy-start(bf16[512,1024]{1,0:T(8,128)(2,1)} %own_codes.1) | copy-start | bytes 3145732
  0.7 6.0 %copy-start.3 = (bf16[2048]{0:T(1024)(128)(2,1)S(1)}, bf16[2048]{0:T(1024)(128)(2,1)}, u32[]{:S(2)}) copy-start(bf16[2048]{0:T(1024)(128)(2,1)} %param.7) | copy-start | bytes 12292
  0.7 7.6 %collective-permute-start = (bf16[2048,1024]{1,0:T(8,128)(2,1)}, bf16[2048,1024]{1,0:T(8,128)(2,1)}, u32[]{:S(2)}, u32[]{:S(2)}) collective-permute-start(bf16[2048,1024]{1,0:T(8,128)(2,1)} %own_raw.1), channel_id=1, source_target_pairs={{0,1},{1,0},{2,3},{3,2},{4,5},{5,4},{6,7},{7,6},{8,9},{9,8},{10,11... | collective-permute-start | bytes 12582920 | tf_op jit(solution)/shard_map/ppermute | solution.py:30
  2.4 21.5 %collective-permute-start.3 = (bf16[272,1024]{1,0:T(8,128)(2,1)S(1)}, bf16[272,1024]{1,0:T(8,128)(2,1)S(1)}, u32[]{:S(2)}, u32[]{:S(2)}) collective-permute-start(bf16[272,1024]{1,0:T(8,128)(2,1)S(1)} %pad_maximum_fusion), channel_id=1, source_target_pairs={{0,2},{1,3},{2,4},{3,5},{4,6},{5,7},{6,8},{7,9},{8,10},{9,11},{10,... | collective-permute-start | bytes 1671176 | tf_op jit(solution)/shard_map/ppermute | solution.py:25
  5.1 28.6 %collective-permute-start.2 = (bf16[256,1024]{1,0:T(8,128)(2,1)S(1)}, bf16[256,1024]{1,0:T(8,128)(2,1)S(1)}, u32[]{:S(2)}, u32[]{:S(2)}) collective-permute-start(bf16[256,1024]{1,0:T(8,128)(2,1)S(1)} %slice.15), channel_id=1, source_target_pairs={{0,2},{1,3},{2,4},{3,5},{4,6},{5,7},{6,8},{7,9},{8,10},{9,11},{10,... | collective-permute-start | bytes 1572872 | tf_op jit(solution)/shard_map/ppermute | solution.py:25
  6.6 1.3 %collective-permute-start.1 = (bf16[2048]{0:T(1024)(128)(2,1)S(1)}, bf16[2048]{0:T(1024)(128)(2,1)S(1)}, u32[]{:S(2)}, u32[]{:S(2)}) collective-permute-start(bf16[2048]{0:T(1024)(128)(2,1)S(1)} %copy-done.3), channel_id=1, source_target_pairs={{0,1},{1,0},{2,3},{3,2},{4,5},{5,4},{6,7},{7,6},{8,9},{9,8},{10,11... | collective-permute-start | bytes 12296 | tf_op jit(solution)/shard_map/ppermute | solution.py:30
  8.3 2.2 %copy-start.1 = (bf16[2048,1024]{1,0:T(8,128)(2,1)S(1)}, bf16[2048,1024]{1,0:T(8,128)(2,1)}, u32[]{:S(2)}) copy-start(bf16[2048,1024]{1,0:T(8,128)(2,1)} %own_raw.1) | copy-start | bytes 12582916
  26.8 18.0 %collective-permute-start.5 = (bf16[256,1024]{1,0:T(8,128)(2,1)S(1)}, bf16[256,1024]{1,0:T(8,128)(2,1)S(1)}, u32[]{:S(2)}, u32[]{:S(2)}) collective-permute-start(bf16[256,1024]{1,0:T(8,128)(2,1)S(1)} %get-tuple-element.34), channel_id=1, source_target_pairs={{0,30},{1,31},{2,0},{3,1},{4,2},{5,3},{6,4},{7,5},{8,6},{9,7},{10,... | collective-permute-start | bytes 1572872 | tf_op jit(solution)/shard_map/ppermute | solution.py:25
  36.6 17.3 %collective-permute-start.4 = (bf16[256,1024]{1,0:T(8,128)(2,1)S(1)}, bf16[256,1024]{1,0:T(8,128)(2,1)S(1)}, u32[]{:S(2)}, u32[]{:S(2)}) collective-permute-start(bf16[256,1024]{1,0:T(8,128)(2,1)S(1)} %get-tuple-element.32), channel_id=1, source_target_pairs={{0,30},{1,31},{2,0},{3,1},{4,2},{5,3},{6,4},{7,5},{8,6},{9,7},{10,... | collective-permute-start | bytes 1572872 | tf_op jit(solution)/shard_map/ppermute | solution.py:25
  44.7 7.2 %collective-permute-start.6 = (f32[1,2048]{1,0:T(1,128)S(1)}, f32[1,2048]{1,0:T(1,128)S(1)}, u32[]{:S(2)}, u32[]{:S(2)}) collective-permute-start(f32[1,2048]{1,0:T(1,128)S(1)} %get-tuple-element.37), channel_id=1, source_target_pairs={{0,1},{1,0},{2,3},{3,2},{4,5},{5,4},{6,7},{7,6},{8,9},{9,8},{10,11... | collective-permute-start | bytes 24584 | tf_op jit(solution)/shard_map/ppermute | solution.py:30
  44.7 9.1 %collective-permute-start.7 = (f32[1,512]{1,0:T(1,128)S(1)}, f32[1,512]{1,0:T(1,128)S(1)}, u32[]{:S(2)}, u32[]{:S(2)}) collective-permute-start(f32[1,512]{1,0:T(1,128)S(1)} %get-tuple-element.40), channel_id=1, source_target_pairs={{0,30},{1,31},{2,0},{3,1},{4,2},{5,3},{6,4},{7,5},{8,6},{9,7},{10,... | collective-permute-start | bytes 6152 | tf_op jit(solution)/shard_map/ppermute | solution.py:25

commit v6 on v5

--- a/solution.py
+++ b/solution.py
@@ -12,7 +12,7 @@
 EXTRA = 16
 TILE = 1024
 LANES = 128
-NORM = 256
+NORM = 512
 F32 = jnp.float32
 BF16 = jnp.bfloat16
 VMEM = pl.BlockSpec(memory_space=pltpu.VMEM)

time: 55.2 us -> 55.2 us (level)
  no operation moved by 1% of the time
where the time goes in v6:
time: 55.2 us; the launch traced here: 55 us
  Pallas kernels  21.4 us (39%)
  starting transfers between devices  19.7 us (36%)
  waiting for transfers between devices  9.05 us (16%)
  local copies, waits for them, and re-layouts  2.24 us (4%)
  other arithmetic  1.83 us (3%)
  between operations  0.75 us (1%)
    ppermute x5, starting transfers between devices, shift(): lax.ppermute(value, 'blk', [(i, (i + steps) % count) for i in range(count)])  19.2 us
    pallas_call x1, Pallas kernels, on_device(): call(functools.partial(local_kernel, half), [units, units, ((rows, width)...  13.4 us
    ppermute x5, waiting for transfers between devices, shift(): lax.ppermute(value, 'blk', [(i, (i + steps) % count) for i in range(count)])  7.41 us
    pallas_call x2, Pallas kernels, on_device(): call(functools.partial(moved_kernel, cut), [((part, width), BF16), ((1, r...  5.76 us
    pallas_call x2, Pallas kernels, finish(): pl.pallas_call(functools.partial(last_rows if more else first_rows, cut),...  2.27 us
    unnamed x8, local copies, waits for them, and re-layouts  2.2 us
    ppermute x3, waiting for transfers between devices, partner(): return lax.ppermute(value, 'blk', [(i, i ^ 1) for i in range(count)])  1.65 us
    select_n x1, other arithmetic, on_device(): jnp.where(row < cuts[0].stop, first[:, :rows], centroid_scales)  1.14 us
  transfers between devices with their start and end apart: 8, of which 4 were waited for; matrix products, arithmetic and copies ran while one was open for 3% of the time, Pallas kernels for 37%

profile of v6, /device:TPU:0, one launch (start us, length us, event | category | flops | bytes accessed | tf_op | source)
XLA Modules:
  0.0 55.0 jit_solution(1590366869227965416)
XLA Ops:
  0.6 0.0 copy-start.2
  0.6 0.0 copy-start
  0.7 0.0 copy-start.3
  0.7 0.5 collective-permute-start
  1.2 1.1 %slice_select_fusion = (bf16[272,512]{1,0:T(8,128)(2,1)S(1)}, bf16[272,512]{1,0:T(8,128)(2,1)S(1)}) fusion(bf16[512,1024]{1,0:T(8,128)(2,1)} %own_codes.1, pred[272]{0:T(512)(128)(4,1)S(1)} %iota_compare_fusion, bf16[512]{0:T(512)(128)(2,1)} %param.6), kind=kLoop, calls=%fused_computation.1 | loop fusion | flops 139264 | bytes 1115408 | tf_op jit(solution)/shard_map/jit(_where)/select_n | solution.py:229
  2.3 0.1 pad_maximum_fusion
  2.4 2.6 %collective-permute-start.3 = (bf16[272,1024]{1,0:T(8,128)(2,1)S(1)}, bf16[272,1024]{1,0:T(8,128)(2,1)S(1)}, u32[]{:S(2)}, u32[]{:S(2)}) collective-permute-start(bf16[272,1024]{1,0:T(8,128)(2,1)S(1)} %pad_maximum_fusion), channel_id=1, source_target_pairs={{0,2},{1,3},{2,4},{3,5},{4,6},{5,7},{6,8},{7,9},{8,10},{9,11},{10,... | collective-permute-start | bytes 1671176 | tf_op jit(solution)/shard_map/ppermute | solution.py:25
  5.0 0.0 copy-done
  5.1 1.5 %collective-permute-start.2 = (bf16[256,1024]{1,0:T(8,128)(2,1)S(1)}, bf16[256,1024]{1,0:T(8,128)(2,1)S(1)}, u32[]{:S(2)}, u32[]{:S(2)}) collective-permute-start(bf16[256,1024]{1,0:T(8,128)(2,1)S(1)} %slice.15), channel_id=1, source_target_pairs={{0,2},{1,3},{2,4},{3,5},{4,6},{5,7},{6,8},{7,9},{8,10},{9,11},{10,... | collective-permute-start | bytes 1572872 | tf_op jit(solution)/shard_map/ppermute | solution.py:25
  6.6 0.0 copy-done.3
  6.6 0.0 collective-permute-start.1
  6.6 0.0 copy-done.2
  6.7 1.3 %collective-permute-done.1 = bf16[2048]{0:T(1024)(128)(2,1)S(1)} collective-permute-done((bf16[2048]{0:T(1024)(128)(2,1)S(1)}, bf16[2048]{0:T(1024)(128)(2,1)S(1)}, u32[]{:S(2)}, u32[]{:S(2)}) %collective-permute-start.1) | collective-permute-done | bytes 4128 | tf_op jit(solution)/shard_map/ppermute | solution.py:30
  8.0 0.3 collective-permute-done.other_raw
  8.3 0.0 copy-start.1
  8.3 2.2 %copy-done.1 = bf16[2048,1024]{1,0:T(8,128)(2,1)S(1)} copy-done((bf16[2048,1024]{1,0:T(8,128)(2,1)S(1)}, bf16[2048,1024]{1,0:T(8,128)(2,1)}, u32[]{:S(2)}) %copy-start.1) | copy-done | bytes 4194328
  10.5 13.4 %local.1 = (bf16[2048,1024]{1,0:T(8,128)(2,1)S(1)}, bf16[2048,1024]{1,0:T(8,128)(2,1)S(1)}, f32[512,1024]{1,0:T(8,128)S(1)}, f32[1,512]{1,0:T(1,128)S(1)}, f32[1,2048]{1,0:T(1,128)S(1)}, /*index=5*/f32[1,2048]{1,0:T(1,128)S(1)}) custom-call(s32[1]{0:T(128)} %bitcast.odd, bf16[2048,1024]{1,0:T(8,128)(2,1)S(1)} %copy-done.1, ...), custom_call_target="tpu_custom_call" | custom-call | flops 1000 | bytes 1000 | tf_op jit(solution)/shard_map/local/pallas_call | solution.py:239
  23.9 0.0 collective-permute-done.3.codes.scales
  23.9 2.9 %moved0.1 = (bf16[256,1024]{1,0:T(8,128)(2,1)S(1)}, f32[1,512]{1,0:T(1,128)S(1)}, f32[1,2048]{1,0:T(1,128)S(1)}, f32[1,2048]{1,0:T(1,128)S(1)}) custom-call(s32[1]{0:T(128)} %bitcast.odd, bf16[272,1024]{1,0:T(8,128)(2,1)S(1)} %collective-permute-done.3.codes.scales, bf16[272,1024]{1,0:T(8,128)(2,1)S(1)} %collective-permute-done.3.codes.scales, ...), custom_call_target="tpu_custom_call" | custom-call | flops 1000 | bytes 1000 | tf_op jit(solution)/shard_map/moved0/pallas_call | solution.py:257
  26.8 6.9 %collective-permute-start.5 = (bf16[256,1024]{1,0:T(8,128)(2,1)S(1)}, bf16[256,1024]{1,0:T(8,128)(2,1)S(1)}, u32[]{:S(2)}, u32[]{:S(2)}) collective-permute-start(bf16[256,1024]{1,0:T(8,128)(2,1)S(1)} %get-tuple-element.34), channel_id=1, source_target_pairs={{0,30},{1,31},{2,0},{3,1},{4,2},{5,3},{6,4},{7,5},{8,6},{9,7},{10,... | collective-permute-start | bytes 1572872 | tf_op jit(solution)/shard_map/ppermute | solution.py:25
  33.7 0.0 collective-permute-done.2.codes
  33.7 2.9 %moved1.1 = (bf16[256,1024]{1,0:T(8,128)(2,1)S(1)}, f32[1,512]{1,0:T(1,128)S(1)}, f32[1,2048]{1,0:T(1,128)S(1)}, f32[1,2048]{1,0:T(1,128)S(1)}) custom-call(s32[1]{0:T(128)} %bitcast.odd, bf16[256,1024]{1,0:T(8,128)(2,1)S(1)} %collective-permute-done.2.codes, bf16[272,1024]{1,0:T(8,128)(2,1)S(1)} %collective-permute-done.3.codes.scales, ...), custom_call_target="tpu_custom_call" | custom-call | flops 1000 | bytes 1000 | tf_op jit(solution)/shard_map/moved1/pallas_call | solution.py:257
  36.6 2.1 %collective-permute-start.4 = (bf16[256,1024]{1,0:T(8,128)(2,1)S(1)}, bf16[256,1024]{1,0:T(8,128)(2,1)S(1)}, u32[]{:S(2)}, u32[]{:S(2)}) collective-permute-start(bf16[256,1024]{1,0:T(8,128)(2,1)S(1)} %get-tuple-element.32), channel_id=1, source_target_pairs={{0,30},{1,31},{2,0},{3,1},{4,2},{5,3},{6,4},{7,5},{8,6},{9,7},{10,... | collective-permute-start | bytes 1572872 | tf_op jit(solution)/shard_map/ppermute | solution.py:25
  38.6 6.1 %collective-permute-done.5.back = bf16[256,1024]{1,0:T(8,128)(2,1)S(1)} collective-permute-done((bf16[256,1024]{1,0:T(8,128)(2,1)S(1)}, bf16[256,1024]{1,0:T(8,128)(2,1)S(1)}, u32[]{:S(2)}, u32[]{:S(2)}) %collective-permute-start.5) | collective-permute-done | bytes 524320 | tf_op jit(solution)/shard_map/ppermute | solution.py:25
  44.7 0.0 collective-permute-start.6
  44.7 6.1 %collective-permute-start.7 = (f32[1,512]{1,0:T(1,128)S(1)}, f32[1,512]{1,0:T(1,128)S(1)}, u32[]{:S(2)}, u32[]{:S(2)}) collective-permute-start(f32[1,512]{1,0:T(1,128)S(1)} %get-tuple-element.40), channel_id=1, source_target_pairs={{0,30},{1,31},{2,0},{3,1},{4,2},{5,3},{6,4},{7,5},{8,6},{9,7},{10,... | collective-permute-start | bytes 6152 | tf_op jit(solution)/shard_map/ppermute | solution.py:25
  50.8 1.1 %finish0.1.before = f32[512,1024]{1,0:T(8,128)} custom-call(f32[512,1024]{1,0:T(8,128)S(1)} %get-tuple-element.24.numer, bf16[256,1024]{1,0:T(8,128)(2,1)S(1)} %collective-permute-done.5.back), custom_call_target="tpu_custom_call" | custom-call | flops 1000 | bytes 1000 | tf_op jit(solution)/shard_map/finish0/pallas_call | solution.py:205
  52.0 0.0 collective-permute-done.6
  52.0 0.6 %add_log_fusion = f32[1,2048]{1,0:T(1,128)} fusion(f32[1,2048]{1,0:T(1,128)S(1)} %get-tuple-element.33, f32[1,2048]{1,0:T(1,128)S(1)} %collective-permute-done.6), kind=kLoop, calls=%fused_computation.2 | loop fusion | flops 2048 | bytes 24576 | tf_op jit(solution)/shard_map/log | solution.py:269
  52.6 1.3 %collective-permute-done.4.back = bf16[256,1024]{1,0:T(8,128)(2,1)S(1)} collective-permute-done((bf16[256,1024]{1,0:T(8,128)(2,1)S(1)}, bf16[256,1024]{1,0:T(8,128)(2,1)S(1)}, u32[]{:S(2)}, u32[]{:S(2)}) %collective-permute-start.4) | collective-permute-done | bytes 524320 | tf_op jit(solution)/shard_map/ppermute | solution.py:25
  53.9 0.0 collective-permute-done.7.back_sums
  53.9 1.1 %finish256.1 = (f32[512,1024]{1,0:T(8,128)}, f32[1,512]{1,0:T(1,128)}) custom-call(f32[512,1024]{1,0:T(8,128)S(1)} %get-tuple-element.24.numer, bf16[256,1024]{1,0:T(8,128)(2,1)S(1)} %collective-permute-done.4.back, f32[1,512]{1,0:T(1,128)S(1)} %get-tuple-element.39.sums, ...), custom_call_target="tpu_custom_call", output_to_operand_aliasing={{0}: (4, {})} | custom-call | flops 1000 | bytes 1000 | tf_op jit(solution)/shard_map/finish256/pallas_call | solution.py:205
  (6 shorter events, 0.1 us)
Async XLA Ops:
  0.6 6.0 %copy-start.2 = (bf16[512]{0:T(512)(128)(2,1)S(1)}, bf16[512]{0:T(512)(128)(2,1)}, u32[]{:S(2)}) copy-start(bf16[512]{0:T(512)(128)(2,1)} %param.6) | copy-start | bytes 3076
  0.6 4.4 %copy-start = (bf16[512,1024]{1,0:T(8,128)(2,1)S(1)}, bf16[512,1024]{1,0:T(8,128)(2,1)}, u32[]{:S(2)}) copy-start(bf16[512,1024]{1,0:T(8,128)(2,1)} %own_codes.1) | copy-start | bytes 3145732
  0.7 6.0 %copy-start.3 = (bf16[2048]{0:T(1024)(128)(2,1)S(1)}, bf16[2048]{0:T(1024)(128)(2,1)}, u32[]{:S(2)}) copy-start(bf16[2048]{0:T(1024)(128)(2,1)} %param.7) | copy-start | bytes 12292
  0.7 7.6 %collective-permute-start = (bf16[2048,1024]{1,0:T(8,128)(2,1)}, bf16[2048,1024]{1,0:T(8,128)(2,1)}, u32[]{:S(2)}, u32[]{:S(2)}) collective-permute-start(bf16[2048,1024]{1,0:T(8,128)(2,1)} %own_raw.1), channel_id=1, source_target_pairs={{0,1},{1,0},{2,3},{3,2},{4,5},{5,4},{6,7},{7,6},{8,9},{9,8},{10,11... | collective-permute-start | bytes 12582920 | tf_op jit(solution)/shard_map/ppermute | solution.py:30
  2.4 21.5 %collective-permute-start.3 = (bf16[272,1024]{1,0:T(8,128)(2,1)S(1)}, bf16[272,1024]{1,0:T(8,128)(2,1)S(1)}, u32[]{:S(2)}, u32[]{:S(2)}) collective-permute-start(bf16[272,1024]{1,0:T(8,128)(2,1)S(1)} %pad_maximum_fusion), channel_id=1, source_target_pairs={{0,2},{1,3},{2,4},{3,5},{4,6},{5,7},{6,8},{7,9},{8,10},{9,11},{10,... | collective-permute-start | bytes 1671176 | tf_op jit(solution)/shard_map/ppermute | solution.py:25
  5.1 28.6 %collective-permute-start.2 = (bf16[256,1024]{1,0:T(8,128)(2,1)S(1)}, bf16[256,1024]{1,0:T(8,128)(2,1)S(1)}, u32[]{:S(2)}, u32[]{:S(2)}) collective-permute-start(bf16[256,1024]{1,0:T(8,128)(2,1)S(1)} %slice.15), channel_id=1, source_target_pairs={{0,2},{1,3},{2,4},{3,5},{4,6},{5,7},{6,8},{7,9},{8,10},{9,11},{10,... | collective-permute-start | bytes 1572872 | tf_op jit(solution)/shard_map/ppermute | solution.py:25
  6.6 1.3 %collective-permute-start.1 = (bf16[2048]{0:T(1024)(128)(2,1)S(1)}, bf16[2048]{0:T(1024)(128)(2,1)S(1)}, u32[]{:S(2)}, u32[]{:S(2)}) collective-permute-start(bf16[2048]{0:T(1024)(128)(2,1)S(1)} %copy-done.3), channel_id=1, source_target_pairs={{0,1},{1,0},{2,3},{3,2},{4,5},{5,4},{6,7},{7,6},{8,9},{9,8},{10,11... | collective-permute-start | bytes 12296 | tf_op jit(solution)/shard_map/ppermute | solution.py:30
  8.3 2.2 %copy-start.1 = (bf16[2048,1024]{1,0:T(8,128)(2,1)S(1)}, bf16[2048,1024]{1,0:T(8,128)(2,1)}, u32[]{:S(2)}) copy-start(bf16[2048,1024]{1,0:T(8,128)(2,1)} %own_raw.1) | copy-start | bytes 12582916
  26.8 18.0 %collective-permute-start.5 = (bf16[256,1024]{1,0:T(8,128)(2,1)S(1)}, bf16[256,1024]{1,0:T(8,128)(2,1)S(1)}, u32[]{:S(2)}, u32[]{:S(2)}) collective-permute-start(bf16[256,1024]{1,0:T(8,128)(2,1)S(1)} %get-tuple-element.34), channel_id=1, source_target_pairs={{0,30},{1,31},{2,0},{3,1},{4,2},{5,3},{6,4},{7,5},{8,6},{9,7},{10,... | collective-permute-start | bytes 1572872 | tf_op jit(solution)/shard_map/ppermute | solution.py:25
  36.6 17.3 %collective-permute-start.4 = (bf16[256,1024]{1,0:T(8,128)(2,1)S(1)}, bf16[256,1024]{1,0:T(8,128)(2,1)S(1)}, u32[]{:S(2)}, u32[]{:S(2)}) collective-permute-start(bf16[256,1024]{1,0:T(8,128)(2,1)S(1)} %get-tuple-element.32), channel_id=1, source_target_pairs={{0,30},{1,31},{2,0},{3,1},{4,2},{5,3},{6,4},{7,5},{8,6},{9,7},{10,... | collective-permute-start | bytes 1572872 | tf_op jit(solution)/shard_map/ppermute | solution.py:25
  44.7 7.2 %collective-permute-start.6 = (f32[1,2048]{1,0:T(1,128)S(1)}, f32[1,2048]{1,0:T(1,128)S(1)}, u32[]{:S(2)}, u32[]{:S(2)}) collective-permute-start(f32[1,2048]{1,0:T(1,128)S(1)} %get-tuple-element.37), channel_id=1, source_target_pairs={{0,1},{1,0},{2,3},{3,2},{4,5},{5,4},{6,7},{7,6},{8,9},{9,8},{10,11... | collective-permute-start | bytes 24584 | tf_op jit(solution)/shard_map/ppermute | solution.py:30
  44.7 9.1 %collective-permute-start.7 = (f32[1,512]{1,0:T(1,128)S(1)}, f32[1,512]{1,0:T(1,128)S(1)}, u32[]{:S(2)}, u32[]{:S(2)}) collective-permute-start(f32[1,512]{1,0:T(1,128)S(1)} %get-tuple-element.40), channel_id=1, source_target_pairs={{0,30},{1,31},{2,0},{3,1},{4,2},{5,3},{6,4},{7,5},{8,6},{9,7},{10,... | collective-permute-start | bytes 6152 | tf_op jit(solution)/shard_map/ppermute | solution.py:25

commit v7 on v5

--- a/solution.py
+++ b/solution.py
@@ -10,7 +10,7 @@
 HALVES = 2
 SIZES = (256, 256)
 EXTRA = 16
-TILE = 1024
+TILE = 2048
 LANES = 128
 NORM = 256
 F32 = jnp.float32

time: 55.2 us -> 55.1 us (level)
  transfers between devices with their start and end apart: 8 -> 8, of which waited for: 4 -> 5; matrix products, arithmetic and copies ran while one was open for 3% -> 3% of each run, Pallas kernels for 37% -> 36%
where the time goes in v7:
time: 55.1 us; the launch traced here: 55 us
  Pallas kernels  21 us (38%)
  starting transfers between devices  19.9 us (36%)
  waiting for transfers between devices  9.28 us (17%)
  local copies, waits for them, and re-layouts  2.24 us (4%)
  other arithmetic  1.83 us (3%)
  between operations  0.75 us (1%)
    ppermute x5, starting transfers between devices, shift(): lax.ppermute(value, 'blk', [(i, (i + steps) % count) for i in range(count)])  19.3 us
    pallas_call x1, Pallas kernels, on_device(): call(functools.partial(local_kernel, half), [units, units, ((rows, width)...  12.9 us
    ppermute x5, waiting for transfers between devices, shift(): lax.ppermute(value, 'blk', [(i, (i + steps) % count) for i in range(count)])  7.63 us
    pallas_call x2, Pallas kernels, on_device(): call(functools.partial(moved_kernel, cut), [((part, width), BF16), ((1, r...  5.77 us
    pallas_call x2, Pallas kernels, finish(): pl.pallas_call(functools.partial(last_rows if more else first_rows, cut),...  2.27 us
    unnamed x8, local copies, waits for them, and re-layouts  2.2 us
    ppermute x3, waiting for transfers between devices, partner(): return lax.ppermute(value, 'blk', [(i, i ^ 1) for i in range(count)])  1.65 us
    select_n x1, other arithmetic, on_device(): jnp.where(row < cuts[0].stop, first[:, :rows], centroid_scales)  1.14 us
  transfers between devices with their start and end apart: 8, of which 5 were waited for; matrix products, arithmetic and copies ran while one was open for 3% of the time, Pallas kernels for 36%

profile of v7, /device:TPU:0, one launch (start us, length us, event | category | flops | bytes accessed | tf_op | source)
XLA Modules:
  0.0 55.0 jit_solution(5293082773130869641)
XLA Ops:
  0.6 0.0 copy-start.2
  0.6 0.0 copy-start
  0.7 0.0 copy-start.3
  0.7 0.5 collective-permute-start
  1.2 1.1 %slice_select_fusion = (bf16[272,512]{1,0:T(8,128)(2,1)S(1)}, bf16[272,512]{1,0:T(8,128)(2,1)S(1)}) fusion(bf16[512,1024]{1,0:T(8,128)(2,1)} %own_codes.1, pred[272]{0:T(512)(128)(4,1)S(1)} %iota_compare_fusion, bf16[512]{0:T(512)(128)(2,1)} %param.6), kind=kLoop, calls=%fused_computation.1 | loop fusion | flops 139264 | bytes 1115408 | tf_op jit(solution)/shard_map/jit(_where)/select_n | solution.py:229
  2.3 0.1 pad_maximum_fusion
  2.4 2.6 %collective-permute-start.3 = (bf16[272,1024]{1,0:T(8,128)(2,1)S(1)}, bf16[272,1024]{1,0:T(8,128)(2,1)S(1)}, u32[]{:S(2)}, u32[]{:S(2)}) collective-permute-start(bf16[272,1024]{1,0:T(8,128)(2,1)S(1)} %pad_maximum_fusion), channel_id=1, source_target_pairs={{0,2},{1,3},{2,4},{3,5},{4,6},{5,7},{6,8},{7,9},{8,10},{9,11},{10,... | collective-permute-start | bytes 1671176 | tf_op jit(solution)/shard_map/ppermute | solution.py:25
  5.0 0.0 copy-done
  5.1 1.5 %collective-permute-start.2 = (bf16[256,1024]{1,0:T(8,128)(2,1)S(1)}, bf16[256,1024]{1,0:T(8,128)(2,1)S(1)}, u32[]{:S(2)}, u32[]{:S(2)}) collective-permute-start(bf16[256,1024]{1,0:T(8,128)(2,1)S(1)} %slice.15), channel_id=1, source_target_pairs={{0,2},{1,3},{2,4},{3,5},{4,6},{5,7},{6,8},{7,9},{8,10},{9,11},{10,... | collective-permute-start | bytes 1572872 | tf_op jit(solution)/shard_map/ppermute | solution.py:25
  6.6 0.0 copy-done.3
  6.6 0.0 collective-permute-start.1
  6.6 0.0 copy-done.2
  6.7 1.3 %collective-permute-done.1 = bf16[2048]{0:T(1024)(128)(2,1)S(1)} collective-permute-done((bf16[2048]{0:T(1024)(128)(2,1)S(1)}, bf16[2048]{0:T(1024)(128)(2,1)S(1)}, u32[]{:S(2)}, u32[]{:S(2)}) %collective-permute-start.1) | collective-permute-done | bytes 4128 | tf_op jit(solution)/shard_map/ppermute | solution.py:30
  8.0 0.3 collective-permute-done.other_raw
  8.3 0.0 copy-start.1
  8.3 2.2 %copy-done.1 = bf16[2048,1024]{1,0:T(8,128)(2,1)S(1)} copy-done((bf16[2048,1024]{1,0:T(8,128)(2,1)S(1)}, bf16[2048,1024]{1,0:T(8,128)(2,1)}, u32[]{:S(2)}) %copy-start.1) | copy-done | bytes 4194328
  10.5 12.9 %local.1 = (bf16[2048,1024]{1,0:T(8,128)(2,1)S(1)}, bf16[2048,1024]{1,0:T(8,128)(2,1)S(1)}, f32[512,1024]{1,0:T(8,128)S(1)}, f32[1,512]{1,0:T(1,128)S(1)}, f32[1,2048]{1,0:T(1,128)S(1)}, /*index=5*/f32[1,2048]{1,0:T(1,128)S(1)}) custom-call(s32[1]{0:T(128)} %bitcast.odd, bf16[2048,1024]{1,0:T(8,128)(2,1)S(1)} %copy-done.1, ...), custom_call_target="tpu_custom_call" | custom-call | flops 1000 | bytes 1000 | tf_op jit(solution)/shard_map/local/pallas_call | solution.py:239
  23.4 0.0 collective-permute-done.3.codes.scales
  23.5 2.9 %moved0.1 = (bf16[256,1024]{1,0:T(8,128)(2,1)S(1)}, f32[1,512]{1,0:T(1,128)S(1)}, f32[1,2048]{1,0:T(1,128)S(1)}, f32[1,2048]{1,0:T(1,128)S(1)}) custom-call(s32[1]{0:T(128)} %bitcast.odd, bf16[272,1024]{1,0:T(8,128)(2,1)S(1)} %collective-permute-done.3.codes.scales, bf16[272,1024]{1,0:T(8,128)(2,1)S(1)} %collective-permute-done.3.codes.scales, ...), custom_call_target="tpu_custom_call" | custom-call | flops 1000 | bytes 1000 | tf_op jit(solution)/shard_map/moved0/pallas_call | solution.py:257
  26.4 6.9 %collective-permute-start.5 = (bf16[256,1024]{1,0:T(8,128)(2,1)S(1)}, bf16[256,1024]{1,0:T(8,128)(2,1)S(1)}, u32[]{:S(2)}, u32[]{:S(2)}) collective-permute-start(bf16[256,1024]{1,0:T(8,128)(2,1)S(1)} %get-tuple-element.34), channel_id=1, source_target_pairs={{0,30},{1,31},{2,0},{3,1},{4,2},{5,3},{6,4},{7,5},{8,6},{9,7},{10,... | collective-permute-start | bytes 1572872 | tf_op jit(solution)/shard_map/ppermute | solution.py:25
  33.3 0.3 collective-permute-done.2.codes
  33.6 2.9 %moved1.1 = (bf16[256,1024]{1,0:T(8,128)(2,1)S(1)}, f32[1,512]{1,0:T(1,128)S(1)}, f32[1,2048]{1,0:T(1,128)S(1)}, f32[1,2048]{1,0:T(1,128)S(1)}) custom-call(s32[1]{0:T(128)} %bitcast.odd, bf16[256,1024]{1,0:T(8,128)(2,1)S(1)} %collective-permute-done.2.codes, bf16[272,1024]{1,0:T(8,128)(2,1)S(1)} %collective-permute-done.3.codes.scales, ...), custom_call_target="tpu_custom_call" | custom-call | flops 1000 | bytes 1000 | tf_op jit(solution)/shard_map/moved1/pallas_call | solution.py:257
  36.5 2.2 %collective-permute-start.4 = (bf16[256,1024]{1,0:T(8,128)(2,1)S(1)}, bf16[256,1024]{1,0:T(8,128)(2,1)S(1)}, u32[]{:S(2)}, u32[]{:S(2)}) collective-permute-start(bf16[256,1024]{1,0:T(8,128)(2,1)S(1)} %get-tuple-element.32), channel_id=1, source_target_pairs={{0,30},{1,31},{2,0},{3,1},{4,2},{5,3},{6,4},{7,5},{8,6},{9,7},{10,... | collective-permute-start | bytes 1572872 | tf_op jit(solution)/shard_map/ppermute | solution.py:25
  38.6 5.9 %collective-permute-done.5.back = bf16[256,1024]{1,0:T(8,128)(2,1)S(1)} collective-permute-done((bf16[256,1024]{1,0:T(8,128)(2,1)S(1)}, bf16[256,1024]{1,0:T(8,128)(2,1)S(1)}, u32[]{:S(2)}, u32[]{:S(2)}) %collective-permute-start.5) | collective-permute-done | bytes 524320 | tf_op jit(solution)/shard_map/ppermute | solution.py:25
  44.6 0.0 collective-permute-start.6
  44.6 6.1 %collective-permute-start.7 = (f32[1,512]{1,0:T(1,128)S(1)}, f32[1,512]{1,0:T(1,128)S(1)}, u32[]{:S(2)}, u32[]{:S(2)}) collective-permute-start(f32[1,512]{1,0:T(1,128)S(1)} %get-tuple-element.40), channel_id=1, source_target_pairs={{0,30},{1,31},{2,0},{3,1},{4,2},{5,3},{6,4},{7,5},{8,6},{9,7},{10,... | collective-permute-start | bytes 6152 | tf_op jit(solution)/shard_map/ppermute | solution.py:25
  50.7 1.1 %finish0.1.before = f32[512,1024]{1,0:T(8,128)} custom-call(f32[512,1024]{1,0:T(8,128)S(1)} %get-tuple-element.24.numer, bf16[256,1024]{1,0:T(8,128)(2,1)S(1)} %collective-permute-done.5.back), custom_call_target="tpu_custom_call" | custom-call | flops 1000 | bytes 1000 | tf_op jit(solution)/shard_map/finish0/pallas_call | solution.py:205
  51.8 0.0 collective-permute-done.6
  51.8 0.6 %add_log_fusion = f32[1,2048]{1,0:T(1,128)} fusion(f32[1,2048]{1,0:T(1,128)S(1)} %get-tuple-element.33, f32[1,2048]{1,0:T(1,128)S(1)} %collective-permute-done.6), kind=kLoop, calls=%fused_computation.2 | loop fusion | flops 2048 | bytes 24576 | tf_op jit(solution)/shard_map/log | solution.py:269
  52.4 1.4 %collective-permute-done.4.back = bf16[256,1024]{1,0:T(8,128)(2,1)S(1)} collective-permute-done((bf16[256,1024]{1,0:T(8,128)(2,1)S(1)}, bf16[256,1024]{1,0:T(8,128)(2,1)S(1)}, u32[]{:S(2)}, u32[]{:S(2)}) %collective-permute-start.4) | collective-permute-done | bytes 524320 | tf_op jit(solution)/shard_map/ppermute | solution.py:25
  53.8 0.0 collective-permute-done.7.back_sums
  53.8 1.1 %finish256.1 = (f32[512,1024]{1,0:T(8,128)}, f32[1,512]{1,0:T(1,128)}) custom-call(f32[512,1024]{1,0:T(8,128)S(1)} %get-tuple-element.24.numer, bf16[256,1024]{1,0:T(8,128)(2,1)S(1)} %collective-permute-done.4.back, f32[1,512]{1,0:T(1,128)S(1)} %get-tuple-element.39.sums, ...), custom_call_target="tpu_custom_call", output_to_operand_aliasing={{0}: (4, {})} | custom-call | flops 1000 | bytes 1000 | tf_op jit(solution)/shard_map/finish256/pallas_call | solution.py:205
  (6 shorter events, 0.1 us)
Async XLA Ops:
  0.6 6.0 %copy-start.2 = (bf16[512]{0:T(512)(128)(2,1)S(1)}, bf16[512]{0:T(512)(128)(2,1)}, u32[]{:S(2)}) copy-start(bf16[512]{0:T(512)(128)(2,1)} %param.6) | copy-start | bytes 3076
  0.6 4.4 %copy-start = (bf16[512,1024]{1,0:T(8,128)(2,1)S(1)}, bf16[512,1024]{1,0:T(8,128)(2,1)}, u32[]{:S(2)}) copy-start(bf16[512,1024]{1,0:T(8,128)(2,1)} %own_codes.1) | copy-start | bytes 3145732
  0.7 6.0 %copy-start.3 = (bf16[2048]{0:T(1024)(128)(2,1)S(1)}, bf16[2048]{0:T(1024)(128)(2,1)}, u32[]{:S(2)}) copy-start(bf16[2048]{0:T(1024)(128)(2,1)} %param.7) | copy-start | bytes 12292
  0.7 7.6 %collective-permute-start = (bf16[2048,1024]{1,0:T(8,128)(2,1)}, bf16[2048,1024]{1,0:T(8,128)(2,1)}, u32[]{:S(2)}, u32[]{:S(2)}) collective-permute-start(bf16[2048,1024]{1,0:T(8,128)(2,1)} %own_raw.1), channel_id=1, source_target_pairs={{0,1},{1,0},{2,3},{3,2},{4,5},{5,4},{6,7},{7,6},{8,9},{9,8},{10,11... | collective-permute-start | bytes 12582920 | tf_op jit(solution)/shard_map/ppermute | solution.py:30
  2.4 21.0 %collective-permute-start.3 = (bf16[272,1024]{1,0:T(8,128)(2,1)S(1)}, bf16[272,1024]{1,0:T(8,128)(2,1)S(1)}, u32[]{:S(2)}, u32[]{:S(2)}) collective-permute-start(bf16[272,1024]{1,0:T(8,128)(2,1)S(1)} %pad_maximum_fusion), channel_id=1, source_target_pairs={{0,2},{1,3},{2,4},{3,5},{4,6},{5,7},{6,8},{7,9},{8,10},{9,11},{10,... | collective-permute-start | bytes 1671176 | tf_op jit(solution)/shard_map/ppermute | solution.py:25
  5.1 28.5 %collective-permute-start.2 = (bf16[256,1024]{1,0:T(8,128)(2,1)S(1)}, bf16[256,1024]{1,0:T(8,128)(2,1)S(1)}, u32[]{:S(2)}, u32[]{:S(2)}) collective-permute-start(bf16[256,1024]{1,0:T(8,128)(2,1)S(1)} %slice.15), channel_id=1, source_target_pairs={{0,2},{1,3},{2,4},{3,5},{4,6},{5,7},{6,8},{7,9},{8,10},{9,11},{10,... | collective-permute-start | bytes 1572872 | tf_op jit(solution)/shard_map/ppermute | solution.py:25
  6.6 1.3 %collective-permute-start.1 = (bf16[2048]{0:T(1024)(128)(2,1)S(1)}, bf16[2048]{0:T(1024)(128)(2,1)S(1)}, u32[]{:S(2)}, u32[]{:S(2)}) collective-permute-start(bf16[2048]{0:T(1024)(128)(2,1)S(1)} %copy-done.3), channel_id=1, source_target_pairs={{0,1},{1,0},{2,3},{3,2},{4,5},{5,4},{6,7},{7,6},{8,9},{9,8},{10,11... | collective-permute-start | bytes 12296 | tf_op jit(solution)/shard_map/ppermute | solution.py:30
  8.3 2.2 %copy-start.1 = (bf16[2048,1024]{1,0:T(8,128)(2,1)S(1)}, bf16[2048,1024]{1,0:T(8,128)(2,1)}, u32[]{:S(2)}) copy-start(bf16[2048,1024]{1,0:T(8,128)(2,1)} %own_raw.1) | copy-start | bytes 12582916
  26.4 18.2 %collective-permute-start.5 = (bf16[256,1024]{1,0:T(8,128)(2,1)S(1)}, bf16[256,1024]{1,0:T(8,128)(2,1)S(1)}, u32[]{:S(2)}, u32[]{:S(2)}) collective-permute-start(bf16[256,1024]{1,0:T(8,128)(2,1)S(1)} %get-tuple-element.34), channel_id=1, source_target_pairs={{0,30},{1,31},{2,0},{3,1},{4,2},{5,3},{6,4},{7,5},{8,6},{9,7},{10,... | collective-permute-start | bytes 1572872 | tf_op jit(solution)/shard_map/ppermute | solution.py:25
  36.5 17.3 %collective-permute-start.4 = (bf16[256,1024]{1,0:T(8,128)(2,1)S(1)}, bf16[256,1024]{1,0:T(8,128)(2,1)S(1)}, u32[]{:S(2)}, u32[]{:S(2)}) collective-permute-start(bf16[256,1024]{1,0:T(8,128)(2,1)S(1)} %get-tuple-element.32), channel_id=1, source_target_pairs={{0,30},{1,31},{2,0},{3,1},{4,2},{5,3},{6,4},{7,5},{8,6},{9,7},{10,... | collective-permute-start | bytes 1572872 | tf_op jit(solution)/shard_map/ppermute | solution.py:25
  44.6 7.2 %collective-permute-start.6 = (f32[1,2048]{1,0:T(1,128)S(1)}, f32[1,2048]{1,0:T(1,128)S(1)}, u32[]{:S(2)}, u32[]{:S(2)}) collective-permute-start(f32[1,2048]{1,0:T(1,128)S(1)} %get-tuple-element.37), channel_id=1, source_target_pairs={{0,1},{1,0},{2,3},{3,2},{4,5},{5,4},{6,7},{7,6},{8,9},{9,8},{10,11... | collective-permute-start | bytes 24584 | tf_op jit(solution)/shard_map/ppermute | solution.py:30
  44.6 9.2 %collective-permute-start.7 = (f32[1,512]{1,0:T(1,128)S(1)}, f32[1,512]{1,0:T(1,128)S(1)}, u32[]{:S(2)}, u32[]{:S(2)}) collective-permute-start(f32[1,512]{1,0:T(1,128)S(1)} %get-tuple-element.40), channel_id=1, source_target_pairs={{0,30},{1,31},{2,0},{3,1},{4,2},{5,3},{6,4},{7,5},{8,6},{9,7},{10,... | collective-permute-start | bytes 6152 | tf_op jit(solution)/shard_map/ppermute | solution.py:25
